TPU v7x, 32 devices: a whole 2x2x4 slice. The times are simulated.
32 devices in a mesh: sec: 4 (over x, core), space: 8 (over z, y).
Axes of the slice: x: 2, y: 2, z: 4, core: 2. Of those that a mesh axis runs over, the one named last changes fastest.
Arguments:
- droplet_integrals: float32 [64, 5, 64, 2048], P('sec', None, 'space'), may hold values from -3 to 3, as said below
- flow_number_lengthwise: float32 [64], P('sec'), may hold values from -0.6 to 0.6
- flow_number_crosswise: float32 [64], P('sec'), may hold values from -0.35 to 0.35
- inflow_boundary_integrals: float32 [64, 5], P('sec'), may hold values from 0.2 to 2
- boundary_wall_indicator: int32 [64, 2048], P('space'), may hold values 0 or 1
- inflow_indicator: int32 [64, 2048], P('space'), may hold values 0 or 1
- collision_coefficient: float32 [64, 64], replicated, may hold values from 0.0005 to 0.008
- collision_target_share: float32 [64, 64], replicated, may hold values from 0 to 0.03
- evaporation_speed_stepwise: float32 [64], replicated, may hold values from 0.01 to 0.1
- thermal_factor: float32 [64, 2048], P('space', 'sec'), may hold values from 0.5 to 2
Outputs:
- spray: float32 [64, 5, 64, 2048], P(None, None, 'space', 'sec')
- gas_source: float32 [5, 64, 2048], P(None, 'space', 'sec')
Inputs may be any that keep to these rules, and one draw needn't show every extreme that they name: `droplet_integrals`: moment 0 (mass) is positive, 0.1 or more, in every section and cell.
All inputs are finite; a program needn't handle non-finite values. No bound on the sum of `boundary_wall_indicator` or of `inflow_indicator` on one device may be relied on, other than what follows from the above.
Results may differ from a plain program's by a relative error of at most 0.000084.
Values sent between devices are 32-bit elements; how exact they have to be, the bound alone decides.
No kernel may reach another device: no remote copies, remote signals or barrier semaphores. Data moves between devices by JAX's collectives and lax.ppermute only.
A program may use at most 128 MiB of HBM per device.

v0:
```python
import functools

import jax
import jax.numpy as jnp
from jax import lax
from jax.experimental import pallas as pl
from jax.experimental.pallas import tpu as pltpu
from jax.sharding import PartitionSpec as P

SUB = 4
ROWS = 2 * SUB
LANES = 128
TILE = 8
F32 = jnp.float32
BF16 = jnp.bfloat16
PLAN = ((0, "y"), (1, "y"), (2, "z"), (3, "z"), (4, "z"))
SELECT = ((0, 2), (1, 3, 4))
TOGETHER_INNER = 5
TOGETHER_OUTER = 4
VMEM_LIMIT = 48 * 1024 * 1024


def stacked(array):
    *lead, rows, columns = array.shape
    tiles = columns // LANES
    array = array.reshape(*lead, rows, tiles, LANES)
    return jnp.swapaxes(array, -3, -2).reshape(*lead, rows * tiles, LANES)


def sublane(shape=(TILE, LANES)):
    return lax.broadcasted_iota(jnp.int32, shape, 0)


class Wind:
    def __init__(self, speed_x, speed_y, blocks):
        self.a, self.b = jnp.abs(speed_x), jnp.abs(speed_y)
        self.own = 1.0 - self.a - self.b
        self.blocks = blocks
        self.positive_x = speed_x > 0.0
        self.positive_y = speed_y > 0.0
        lane = lax.broadcasted_iota(jnp.int32, (TILE, LANES), 1)
        self.lane_shift = jnp.where(self.positive_y, 1, LANES - 1).astype(jnp.int32)
        self.band_shift = jnp.where(self.positive_y, 1, TILE - 1).astype(jnp.int32)
        self.edge = lane == jnp.where(self.positive_y, 0, LANES - 1)
        self.border = sublane() == jnp.where(self.positive_y, 0, TILE - 1)

    def row(self, u, first, last):
        return jnp.where(self.positive_x, first + u, last - u)

    def block(self, j):
        return jnp.where(self.positive_y, j, self.blocks - 1 - j)


def substeps(chains):
    states = [chain[1] for chain in chains]
    for step in range(1, SUB + 1):
        fresh = []
        for (wind, _, code, value), state in zip(chains, states):
            rows = [None] * step
            for u in range(step, ROWS):
                turned = [pltpu.roll(tile, wind.lane_shift, axis=1) for tile in state[u]]
                wrap = pltpu.roll(turned[-1], wind.band_shift, axis=0)
                behind = [jnp.where(wind.border, 0.0, wrap)] + turned[:-1]
                tiles = []
                for j, tile in enumerate(state[u]):
                    side = jnp.where(wind.edge, behind[j], turned[j])
                    moved = wind.own * tile + wind.a * state[u - 1][j] + wind.b * side
                    kind = code(u, j)
                    tiles.append(jnp.where(kind < 0.0, moved, kind * value))
                rows.append(tiles)
            fresh.append(rows)
        states = fresh
    return states


def keep(wind, state, packed):
    blocks = wind.blocks
    for u in range(SUB, ROWS):
        row = wind.row(u, -SUB, ROWS - 1)
        for j, tile in enumerate(state[u]):
            packed[pl.ds(row * blocks + wind.block(j), TILE, stride=SUB * blocks), :] = tile


def scatter(packed, me, outs):
    share = packed.shape[0] // len(outs)
    for k, (out, spot) in enumerate(outs):
        start = pl.multiple_of((me ^ k) * share, share)
        out[spot] = packed[pl.ds(start, share), :]


def select_kernel(coded, count, blocks, ux_ref, *refs):
    if coded:
        (wall_ref, inflow_ref), refs = refs[:2], refs[2:]
    x_refs, out_refs = refs[:count], refs[count : 2 * count]
    per_step = x_refs[0].shape[0]
    step = pl.program_id(0)
    spacing = blocks * ROWS

    def section(s, carry):
        first = jnp.where(ux_ref[step * per_step + s] > 0.0, SUB, 0)
        for x_ref, out_ref in zip(x_refs, out_refs):
            for row in range(SUB):
                for block in range(blocks):
                    spot = (row * blocks + block) * TILE
                    out_ref[s, spot : spot + TILE, :] = x_ref[
                        s, pl.ds(block * ROWS + first + row, TILE, stride=spacing), :
                    ]
        return carry

    lax.fori_loop(0, per_step, section, 0, unroll=2)
    if coded:
        code_ref = refs[-1]

        @pl.when(step == 0)
        def _():
            for row in range(ROWS):
                for block in range(blocks):
                    spot = (row * blocks + block) * TILE
                    source = pl.ds(block * ROWS + row, TILE, stride=spacing)
                    inflow = jnp.where(inflow_ref[source, :] > 0, 1.0, -1.0)
                    code_ref[spot : spot + TILE, :] = jnp.where(
                        wall_ref[source, :] > 0, 0.0, inflow
                    )


def inner_kernel(moments, blocks, together, me_ref, ux_ref, uy_ref, inflow_ref, code_ref, x_ref, *rest):
    *out_refs, packed = rest
    per_step = x_ref.shape[0]
    step = pl.program_id(0)
    me = me_ref[0]
    spacing = blocks * ROWS
    size = x_ref.shape[1] // moments
    share = out_refs[0].shape[1] // moments

    def section(s, carry):
        number = step * per_step + s
        wind = Wind(ux_ref[number], uy_ref[number], blocks)

        def code(u, j):
            spot = (wind.row(u, 0, ROWS - 1) * blocks + wind.block(j)) * TILE
            return code_ref[pl.ds(pl.multiple_of(spot, TILE), TILE), :]

        for low in range(0, moments, together):
            some = range(low, min(moments, low + together))
            chains = []
            for m in some:
                tiles = [
                    [
                        x_ref[
                            s,
                            pl.ds(
                                m * size + wind.block(j) * ROWS + wind.row(u, 0, ROWS - 1),
                                TILE,
                                stride=spacing,
                            ),
                            :,
                        ]
                        for j in range(blocks)
                    ]
                    for u in range(ROWS)
                ]
                chains.append((wind, tiles, code, inflow_ref[number, m]))
            for m, state in zip(some, substeps(chains)):
                keep(wind, state, packed.at[m])
        for m in range(moments):
            scatter(
                packed.at[m],
                me,
                [(out, (s, slice(m * share, (m + 1) * share))) for out in out_refs],
            )
        return carry

    lax.fori_loop(0, per_step, section, 0)


def outer_kernel(
    moment, halos, blocks, together, me_ref, odd_ref, ux_ref, uy_ref, inflow_ref,
    before_ref, after_ref, code_ref, x_ref, *rest
):
    halo_refs, out_refs, (codes, packed) = rest[:halos], rest[halos:-2], rest[-2:]
    per_step = x_ref.shape[0]
    step = pl.program_id(0)
    me = me_ref[0]
    odd = odd_ref[0]
    spacing = blocks * ROWS
    edge = SUB * blocks * TILE
    codes[:edge] = before_ref[...]
    codes[edge : 2 * edge] = after_ref[...]
    codes[2 * edge :] = code_ref[...]

    def sections(turn, carry):
        chains = []
        for i in range(together):
            s = turn * together + i
            number = step * per_step + s
            wind = Wind(ux_ref[number], uy_ref[number], blocks)
            outside = jnp.where(wind.positive_x, 0, edge)
            second = jnp.logical_xor(wind.positive_x, odd == 1)

            def code(u, j, wind=wind, outside=outside):
                if u < SUB:
                    spot = outside + (wind.row(u, 0, SUB - 1) * blocks + wind.block(j)) * TILE
                else:
                    row = wind.row(u, -SUB, ROWS + SUB - 1)
                    spot = 2 * edge + (row * blocks + wind.block(j)) * TILE
                return codes[pl.ds(pl.multiple_of(spot, TILE), TILE), :]

            tiles = []
            for u in range(ROWS):
                row = []
                for j in range(blocks):
                    if u < SUB:
                        spot = (wind.row(u, 0, SUB - 1) * blocks + wind.block(j)) * TILE
                        spot = pl.ds(pl.multiple_of(spot, TILE), TILE)
                        tile = halo_refs[0][s, spot, :]
                        if halos == 2:
                            tile = jnp.where(second, halo_refs[1][s, spot, :], tile)
                    else:
                        start = wind.block(j) * ROWS + wind.row(u, -SUB, ROWS + SUB - 1)
                        tile = x_ref[s, pl.ds(start, TILE, stride=spacing), :]
                    row.append(tile)
                tiles.append(row)
            chains.append((wind, tiles, code, inflow_ref[number, moment]))
        for i, (chain, state) in enumerate(zip(chains, substeps(chains))):
            keep(chain[0], state, packed.at[i])
        for i in range(together):
            number = step * per_step + turn * together + i
            scatter(packed.at[i], me, [(out, number) for out in out_refs])
        return carry

    lax.fori_loop(0, per_step // together, sections, 0)
    if moment == 0:

        @pl.when(step == 0)
        def _():
            size = out_refs[0].shape[1]
            for number in range(size):
                line = jnp.full((1, LANES), ux_ref[number], F32)
                for out in out_refs:
                    out[size, number : number + 1, :] = line


def split_dot(weights, values):
    high = values.astype(BF16)
    rest = (values - high.astype(F32)).astype(BF16)
    return jnp.dot(
        weights, jnp.concatenate([high, rest, high], axis=0), preferred_element_type=F32
    )


def couple_kernel(first, groups, group_size, blocks, *refs):
    me_ref, rate_ref, share_ref, thermal_ref = refs[:4]
    refs = refs[4:]
    sign_refs, inner, outer = refs[:groups], refs[groups : 2 * groups], refs[2 * groups : 3 * groups]
    refs = refs[3 * groups :]
    if first:
        kernel_ref, spray_ref, gas_ref, merge_ref, *scratch = refs
    else:
        merge_ref, _, _, spray_ref, gas_ref, *scratch = refs
    rest, made, total = scratch
    me = me_ref[0]
    sections = groups * group_size
    size = ROWS * blocks
    half = size // 2
    thermal = [thermal_ref[:half, :], thermal_ref[half:, :]]
    gas = tuple(jnp.zeros((half, LANES), F32) for _ in thermal)
    for k in range(groups):

        def section(s, sums, k=k):
            number = (me ^ k) * group_size + s
            flip = jnp.broadcast_to(sign_refs[k][0, pl.ds(s, 1), :], (half, LANES)) > 0.0
            rate = rate_ref[number]
            one, two = inner[k][s], outer[k][s]
            result = []
            for i, moved in enumerate((jnp.where(flip, two, one), jnp.where(flip, one, two))):
                evaporated = (rate * thermal[i]) * moved
                result.append(sums[i] + evaporated)
                rest[pl.ds(pl.multiple_of(number * size + i * half, half), half), :] = moved - evaporated
            return tuple(result)

        gas = lax.fori_loop(0, group_size, section, gas, unroll=4)
    for i in range(2):
        total[i * half : (i + 1) * half, :] = gas[i]
    for block in range(blocks):
        gas_ref[0, :, block * LANES : (block + 1) * LANES] = total[pl.ds(block, ROWS, stride=blocks), :]
    for row in range(ROWS):
        spots = [pl.ds(row * blocks + block, sections, stride=size) for block in range(blocks)]
        cells = jnp.concatenate([rest[spot, :] for spot in spots], axis=1)
        if first:
            merge = split_dot(kernel_ref[...], cells)
            merge_ref[row] = merge
        else:
            merge = merge_ref[row]
        flux = cells * merge
        result = cells - flux + split_dot(share_ref[...], flux)
        for block, spot in enumerate(spots):
            made[spot, :] = result[:, block * LANES : (block + 1) * LANES]

    def write(s, carry):
        for block in range(blocks):
            spray_ref[s, 0, :, block * LANES : (block + 1) * LANES] = made[
                pl.ds(s * size + block, ROWS, stride=blocks), :
            ]
        return carry

    lax.fori_loop(0, sections, write, 0, unroll=8)


def params(**more):
    return pltpu.CompilerParams(vmem_limit_bytes=VMEM_LIMIT, **more)


def split_weights(weights):
    high = lax.reduce_precision(weights, 8, 7)
    return jnp.concatenate([high, high, weights - high], axis=1).astype(BF16)


def shards(
    droplet_integrals,
    flow_number_lengthwise,
    flow_number_crosswise,
    inflow_boundary_integrals,
    boundary_wall_indicator,
    inflow_indicator,
    collision_coefficient,
    collision_target_share,
    evaporation_speed_stepwise,
    thermal_factor,
):
    x, ux, uy = droplet_integrals, flow_number_lengthwise, flow_number_crosswise
    group_size, moments, rows, columns = x.shape
    groups = lax.axis_size("sec")
    slabs = lax.axis_size("space")
    sections = groups * group_size
    width = columns // groups
    blocks = columns // (TILE * LANES)
    size = columns // LANES * ROWS
    share_size = size // 2 // groups
    assert rows == ROWS and slabs % 2 == 0 and TILE % groups == 0

    me = lax.axis_index("sec").astype(jnp.int32).reshape(1)
    odd = (lax.axis_index("space") % 2).astype(jnp.int32).reshape(1)

    swap = [(i, i ^ 1) for i in range(slabs)]
    outward = [(i, i + 2) for i in range(0, slabs - 2, 2)] + [(i, i - 2) for i in range(3, slabs, 2)]
    inward = [(j, i) for i, j in outward]

    smem = pl.BlockSpec(memory_space=pltpu.SMEM)
    anywhere = pl.BlockSpec(memory_space=pl.ANY)
    cells = stacked(x).reshape(group_size, moments * size, LANES)

    def moment_spec(per_step, moment):
        return pl.BlockSpec((per_step, size, LANES), lambda g: (g, moment, 0))

    chosen = {}
    code = None
    edge = SUB * blocks * TILE
    for some in SELECT:
        coded = code is None
        per_step = group_size // 2
        in_specs, operands = [smem], [ux]
        out_specs = [pl.BlockSpec((per_step, edge, LANES), lambda g: (g, 0, 0))] * len(some)
        out_shape = [jax.ShapeDtypeStruct((group_size, edge, LANES), F32)] * len(some)
        if coded:
            flat = pl.BlockSpec((size, LANES), lambda g: (0, 0))
            in_specs += [flat] * 2
            operands += [stacked(boundary_wall_indicator), stacked(inflow_indicator)]
            out_specs.append(flat)
            out_shape.append(jax.ShapeDtypeStruct((size, LANES), F32))
        made = pl.pallas_call(
            functools.partial(select_kernel, coded, len(some), blocks),
            grid=(group_size // per_step,),
            in_specs=in_specs + [moment_spec(per_step, moment) for moment in some],
            out_specs=out_specs,
            out_shape=out_shape,
            compiler_params=params(),
            cost_estimate=pl.CostEstimate(
                flops=x.size, bytes_accessed=x.size * 6 * len(some) // moments, transcendentals=0
            ),
            name="select_upwind_rows",
        )(*operands, *[cells] * len(some))
        if coded:
            code = made[-1]
        chosen.update(zip(some, made))

    before = lax.ppermute(code[edge:], "space", [(i, i + 1) for i in range(slabs - 1)])
    after = lax.ppermute(code[:edge], "space", [(i + 1, i) for i in range(slabs - 1)])

    per_step = 2
    inner = pl.pallas_call(
        functools.partial(inner_kernel, moments, blocks, TOGETHER_INNER),
        grid=(group_size // per_step,),
        in_specs=[smem] * 4
        + [
            pl.BlockSpec((size, LANES), lambda g: (0, 0)),
            pl.BlockSpec((per_step, moments * size, LANES), lambda g: (g, 0, 0)),
        ],
        out_specs=[pl.BlockSpec((per_step, moments * share_size, LANES), lambda g: (g, 0, 0))]
        * groups,
        out_shape=[jax.ShapeDtypeStruct((group_size, moments * share_size, LANES), F32)] * groups,
        scratch_shapes=[pltpu.VMEM((moments, size // 2, LANES), F32)],
        compiler_params=params(),
        cost_estimate=pl.CostEstimate(
            flops=x.size * 20, bytes_accessed=x.size * 6, transcendentals=0
        ),
        name="transport_inner_rows",
    )(me, ux, uy, inflow_boundary_integrals, code, cells)

    def exchange(parts):
        return [parts[0]] + [
            lax.ppermute(parts[k], "sec", [(i, i ^ k) for i in range(groups)])
            for k in range(1, groups)
        ]

    inner = exchange(inner)

    per_step = group_size // 2
    outer = {}
    for moment, way in PLAN:
        if way == "y":
            near = lax.ppermute(chosen[moment], "space", swap)
            halos = [near, lax.ppermute(near, "space", outward)]
        else:
            far = lax.ppermute(chosen[moment], "space", inward)
            stays = (ux > 0.0) == (odd[0] == 0)
            relayed = jnp.where(stays[:, None, None], chosen[moment], far)
            halos = [lax.ppermute(relayed, "space", swap)]
        length = group_size + (moment == 0)
        flat = pl.BlockSpec((edge, LANES), lambda g: (0, 0))
        parts = pl.pallas_call(
            functools.partial(outer_kernel, moment, len(halos), blocks, TOGETHER_OUTER),
            grid=(group_size // per_step,),
            in_specs=[smem] * 5
            + [flat] * 2
            + [pl.BlockSpec((size, LANES), lambda g: (0, 0)), moment_spec(per_step, moment)]
            + [pl.BlockSpec((per_step, edge, LANES), lambda g: (g, 0, 0))] * len(halos),
            out_specs=[pl.BlockSpec((length, share_size, LANES), lambda g: (0, 0, 0))] * groups,
            out_shape=[jax.ShapeDtypeStruct((length, share_size, LANES), F32)] * groups,
            scratch_shapes=[
                pltpu.VMEM((2 * edge + size, LANES), F32),
                pltpu.VMEM((TOGETHER_OUTER, size // 2, LANES), F32),
            ],
            compiler_params=params(),
            cost_estimate=pl.CostEstimate(
                flops=x.size * 4, bytes_accessed=x.size * 2, transcendentals=0
            ),
            name="transport_outer_rows",
        )(me, odd, ux, uy, inflow_boundary_integrals, before, after, code, cells, *halos)
        outer[moment] = exchange(parts)

    share = split_weights(collision_target_share)
    kernel = split_weights(collision_coefficient)
    step_width = blocks * LANES
    steps = width // step_width
    step_size = ROWS * blocks
    thermal = thermal_factor.reshape(ROWS, steps, blocks, LANES).swapaxes(0, 1)
    thermal = thermal.reshape(steps * step_size, LANES)
    spray_type = jax.ShapeDtypeStruct((sections, moments, rows, width), F32)
    gas_type = jax.ShapeDtypeStruct((moments, rows, width), F32)
    merge_type = jax.ShapeDtypeStruct((rows, sections, width), F32)
    merge_spec = pl.BlockSpec((rows, sections, step_width), lambda j: (0, 0, j))
    spray = gas = merge = None
    for moment in [0] + [moment for moment, _ in PLAN if moment]:
        first = moment == 0
        in_specs = (
            [smem] * 2
            + [
                pl.BlockSpec(share.shape, lambda j: (0, 0)),
                pl.BlockSpec((step_size, LANES), lambda j: (j, 0)),
            ]
            + [pl.BlockSpec((1, share_size, LANES), lambda j: (group_size, 0, 0))] * groups
            + [
                pl.BlockSpec(
                    (group_size, step_size // 2, LANES),
                    lambda j, moment=moment: (0, moment * steps + j, 0),
                )
            ]
            * groups
            + [pl.BlockSpec((group_size, step_size // 2, LANES), lambda j: (0, j, 0))] * groups
        )
        operands = [me, evaporation_speed_stepwise, share, thermal]
        operands += list(outer[0]) + list(inner) + list(outer[moment])
        out_specs = [
            pl.BlockSpec((sections, 1, rows, step_width), lambda j, moment=moment: (0, moment, 0, j)),
            pl.BlockSpec((1, rows, step_width), lambda j, moment=moment: (moment, 0, j)),
        ]
        out_shape = [spray_type, gas_type]
        aliases = {}
        if first:
            in_specs.append(pl.BlockSpec(kernel.shape, lambda j: (0, 0)))
            operands.append(kernel)
            out_specs.append(merge_spec)
            out_shape.append(merge_type)
        else:
            aliases = {len(operands) + 1: 0, len(operands) + 2: 1}
            in_specs += [merge_spec, anywhere, anywhere]
            operands += [merge, spray, gas]
        made = pl.pallas_call(
            functools.partial(couple_kernel, first, groups, group_size, blocks),
            grid=(steps,),
            in_specs=in_specs,
            out_specs=out_specs,
            out_shape=out_shape,
            input_output_aliases=aliases,
            scratch_shapes=[pltpu.VMEM((sections * step_size, LANES), F32)] * 2
            + [pltpu.VMEM((step_size, LANES), F32)],
            compiler_params=params(),
            cost_estimate=pl.CostEstimate(
                flops=sections * rows * width * sections * 2,
                bytes_accessed=sections * rows * width * 12,
                transcendentals=0,
            ),
            name="couple_sections",
        )(*operands)
        if first:
            spray, gas, merge = made
        else:
            spray, gas = made
    return spray, gas


def solution(mesh):
    return jax.shard_map(
        shards,
        mesh=mesh,
        in_specs=(
            P("sec", None, "space", None),
            P("sec"),
            P("sec"),
            P("sec", None),
            P("space", None),
            P("space", None),
            P(),
            P(),
            P(),
            P("space", "sec"),
        ),
        out_specs=(P(None, None, "space", "sec"), P(None, "space", "sec")),
        check_vma=False,
    )
```

profile of v0, /device:TPU:0, one launch (start us, length us, event | category | flops | bytes accessed | tf_op | source)
XLA Modules:
  0.0 135.3 jit_solution(1741333538106889775)
XLA Ops:
  0.6 0.8 copy-done
  1.5 0.8 copy-done.1
  2.3 0.7 copy-done.2
  3.0 1.8 %select_upwind_rows.2 = (f32[16,64,128]{2,1,0:T(8,128)S(1)}, f32[16,64,128]{2,1,0:T(8,128)S(1)}, f32[128,128]{1,0:T(8,128)S(1)}) custom-call(f32[16]{0:T(128)S(1)} %copy-done.2, s32[128,128]{1,0:T(8,128)S(1)} %bitcast.26, s32[128,128]{1,0:T(8,128)S(1)} %bitcast.27, f32[16,640,128]{2,1,0:T(8,128)} %bitcast.28, f32[16,640,128]{2,1,0:T(8,128)} %bitcast.29), custom_call_target="tpu_custom_call" | custom-call | flops 1310720 | bytes 3145728 | tf_op jit(solution)/shard_map/select_upwind_rows/pallas_call | solution.py:370
  4.8 1.4 %collective-permute-start.20 = (f32[16,64,128]{2,1,0:T(8,128)S(1)}, f32[16,64,128]{2,1,0:T(8,128)}, u32[]{:S(2)}, u32[]{:S(2)}) collective-permute-start(f32[16,64,128]{2,1,0:T(8,128)S(1)} %get-tuple-element.62), channel_id=1, source_target_pairs={{2,0},{4,2},{6,4},{1,3},{3,5},{5,7},{10,8},{12,10},{14,12},{9,11},... | collective-permute-start | bytes 1572872 | tf_op jit(solution)/shard_map/ppermute | solution.py:424
  6.2 2.9 %select_upwind_rows.3 = (f32[16,64,128]{2,1,0:T(8,128)}, f32[16,64,128]{2,1,0:T(8,128)S(1)}, f32[16,64,128]{2,1,0:T(8,128)S(1)}) custom-call(f32[16]{0:T(128)S(1)} %copy-done.2, f32[16,640,128]{2,1,0:T(8,128)} %bitcast.30, f32[16,640,128]{2,1,0:T(8,128)} %bitcast.31, f32[16,640,128]{2,1,0:T(8,128)} %bitcast.32), custom_call_target="tpu_custom_call" | custom-call | flops 1310720 | bytes 4718592 | tf_op jit(solution)/shard_map/select_upwind_rows/pallas_call | solution.py:370
  9.1 5.9 %collective-permute-start.25 = (f32[16,64,128]{2,1,0:T(8,128)}, f32[16,64,128]{2,1,0:T(8,128)S(1)}, u32[]{:S(2)}, u32[]{:S(2)}) collective-permute-start(f32[16,64,128]{2,1,0:T(8,128)} %get-tuple-element.67), channel_id=1, source_target_pairs={{0,1},{1,0},{2,3},{3,2},{4,5},{5,4},{6,7},{7,6},{8,9},{9,8},{10,11... | collective-permute-start | bytes 1572872 | tf_op jit(solution)/shard_map/ppermute | solution.py:421
  15.0 1.3 collective-permute-start.10
  16.3 1.3 collective-permute-start.15
  17.6 4.4 %collective-permute-start.2 = (f32[16,64,128]{2,1,0:T(8,128)S(1)}, f32[16,64,128]{2,1,0:T(8,128)S(1)}, u32[]{:S(2)}, u32[]{:S(2)}) collective-permute-start(f32[16,64,128]{2,1,0:T(8,128)S(1)} %get-tuple-element.42), channel_id=1, source_target_pairs={{0,1},{1,0},{2,3},{3,2},{4,5},{5,4},{6,7},{7,6},{8,9},{9,8},{10,11... | collective-permute-start | bytes 1572872 | tf_op jit(solution)/shard_map/ppermute | solution.py:421
  22.1 9.9 %transport_inner_rows.1 = (f32[16,80,128]{2,1,0:T(8,128)S(1)}, f32[16,80,128]{2,1,0:T(8,128)S(1)}, f32[16,80,128]{2,1,0:T(8,128)S(1)}, f32[16,80,128]{2,1,0:T(8,128)S(1)}) custom-call(s32[1]{0:T(128)} %bitcast.me_ref.refs_0_, f32[16]{0:T(128)S(1)} %copy-done.3, f32[16]{0:T(128)S(1)} %copy-done.4, f32[16,5]{1,0:T(8,128)S(1)} %copy.21.inflow_ref, ...), custom_call_target="tpu_custom_call" | custom-call | flops 26214400 | bytes 7864320 | tf_op jit(solution)/shard_map/transport_inner_rows/pallas_call | solution.py:390
  32.1 2.9 %collective-permute-start.26 = (f32[16,64,128]{2,1,0:T(8,128)S(1)}, f32[16,64,128]{2,1,0:T(8,128)S(1)}, u32[]{:S(2)}, u32[]{:S(2)}) collective-permute-start(f32[16,64,128]{2,1,0:T(8,128)S(1)} %collective-permute-done.25.rest_0_), channel_id=1, source_target_pairs={{0,2},{2,4},{4,6},{3,1},{5,3},{7,5},{8,10},{10,12},{12,14},{11,9},... | collective-permute-start | bytes 1572872 | tf_op jit(solution)/shard_map/ppermute | solution.py:422
  35.0 9.3 %collective-permute-done.15 = f32[16,64,128]{2,1,0:T(8,128)} collective-permute-done((f32[16,64,128]{2,1,0:T(8,128)S(1)}, f32[16,64,128]{2,1,0:T(8,128)}, u32[]{:S(2)}, u32[]{:S(2)}) %collective-permute-start.15) | collective-permute-done | bytes 524320 | tf_op jit(solution)/shard_map/ppermute | solution.py:424
  44.3 1.6 %broadcast_select_fusion = (f32[16,64,128]{2,1,0:T(8,128)S(1)}, f32[16,64,128]{2,1,0:T(8,128)S(1)}, f32[16,64,128]{2,1,0:T(8,128)S(1)}) fusion(f32[16,64,128]{2,1,0:T(8,128)S(1)} %get-tuple-element.62, f32[16,64,128]{2,1,0:T(8,128)} %collective-permute-done.20, pred[16]{0:T(512)(128)(4,1)S(1)} %compare_compare_fusion, f32[16,64,128]{2,1,0:T(8,128)S(1)} %get-tuple-element.57, ...), kind=kLoop, calls=%fused_computation | loop fusion | flops 393216 | bytes 4718608 | tf_op jit(solution)/shard_map/jit(_where)/select_n | solution.py:426
  46.0 0.7 collective-permute-start.21
  46.7 1.3 collective-permute-start.1
  48.0 11.9 %collective-permute-done.1.after_ref = f32[64,128]{1,0:T(8,128)S(1)} collective-permute-done((f32[64,128]{1,0:T(8,128)S(1)}, f32[64,128]{1,0:T(8,128)S(1)}, u32[]{:S(2)}, u32[]{:S(2)}) %collective-permute-start.1) | collective-permute-done | bytes 32800 | tf_op jit(solution)/shard_map/ppermute | solution.py:387
  59.9 1.4 %collective-permute-start = (f32[64,128]{1,0:T(8,128)S(1)}, f32[64,128]{1,0:T(8,128)S(1)}, u32[]{:S(2)}, u32[]{:S(2)}) collective-permute-start(f32[64,128]{1,0:T(8,128)S(1)} %get-tuple-element.81), channel_id=1, source_target_pairs={{0,1},{1,2},{2,3},{3,4},{4,5},{5,6},{6,7},{8,9},{9,10},{10,11},{11... | collective-permute-start | bytes 98312 | tf_op jit(solution)/shard_map/ppermute | solution.py:386
  61.3 1.6 %collective-permute-done.before_ref = f32[64,128]{1,0:T(8,128)S(1)} collective-permute-done((f32[64,128]{1,0:T(8,128)S(1)}, f32[64,128]{1,0:T(8,128)S(1)}, u32[]{:S(2)}, u32[]{:S(2)}) %collective-permute-start) | collective-permute-done | bytes 32800 | tf_op jit(solution)/shard_map/ppermute | solution.py:386
  62.9 1.3 collective-permute-start.8
  64.2 7.2 %collective-permute-start.3 = (f32[16,64,128]{2,1,0:T(8,128)S(1)}, f32[16,64,128]{2,1,0:T(8,128)S(1)}, u32[]{:S(2)}, u32[]{:S(2)}) collective-permute-start(f32[16,64,128]{2,1,0:T(8,128)S(1)} %collective-permute-done.2.rest_0_), channel_id=1, source_target_pairs={{0,2},{2,4},{4,6},{3,1},{5,3},{7,5},{8,10},{10,12},{12,14},{11,9},... | collective-permute-start | bytes 1572872 | tf_op jit(solution)/shard_map/ppermute | solution.py:422
  71.5 2.0 %collective-permute-start.11 = (f32[16,64,128]{2,1,0:T(8,128)S(1)}, f32[16,64,128]{2,1,0:T(8,128)S(1)}, u32[]{:S(2)}, u32[]{:S(2)}) collective-permute-start(f32[16,64,128]{2,1,0:T(8,128)S(1)} %get-tuple-element.88), channel_id=1, source_target_pairs={{0,1},{1,0},{2,3},{3,2},{4,5},{5,4},{6,7},{7,6},{8,9},{9,8},{10,11... | collective-permute-start | bytes 1572872 | tf_op jit(solution)/shard_map/ppermute | solution.py:427
  73.5 3.3 %transport_outer_rows.9 = (f32[16,16,128]{2,1,0:T(8,128)S(1)}, f32[16,16,128]{2,1,0:T(8,128)S(1)}, f32[16,16,128]{2,1,0:T(8,128)S(1)}, f32[16,16,128]{2,1,0:T(8,128)S(1)}) custom-call(s32[1]{0:T(128)} %bitcast.me_ref.refs_0_, s32[1]{0:T(128)} %bitcast.4.odd_ref, f32[16]{0:T(128)S(1)} %copy-done.3, f32[16]{0:T(128)S(1)} %copy-done.4, ...), custom_call_target="tpu_custom_call" | custom-call | flops 5242880 | bytes 2621440 | tf_op jit(solution)/shard_map/transport_outer_rows/pallas_call | solution.py:430
  76.8 3.3 %transport_outer_rows.8 = (f32[16,16,128]{2,1,0:T(8,128)S(1)}, f32[16,16,128]{2,1,0:T(8,128)S(1)}, f32[16,16,128]{2,1,0:T(8,128)S(1)}, f32[16,16,128]{2,1,0:T(8,128)S(1)}) custom-call(s32[1]{0:T(128)} %bitcast.me_ref.refs_0_, s32[1]{0:T(128)} %bitcast.4.odd_ref, f32[16]{0:T(128)S(1)} %copy-done.3, f32[16]{0:T(128)S(1)} %copy-done.4, ...), custom_call_target="tpu_custom_call" | custom-call | flops 5242880 | bytes 2621440 | tf_op jit(solution)/shard_map/transport_outer_rows/pallas_call | solution.py:430
  80.1 0.5 collective-permute-done.8.refs_10_
  80.6 9.2 %collective-permute-done.9.refs_11_ = f32[16,80,128]{2,1,0:T(8,128)S(1)} collective-permute-done((f32[16,80,128]{2,1,0:T(8,128)S(1)}, f32[16,80,128]{2,1,0:T(8,128)S(1)}, u32[]{:S(2)}, u32[]{:S(2)}) %collective-permute-start.9) | collective-permute-done | bytes 655392 | tf_op jit(solution)/shard_map/ppermute | solution.py:411
  89.7 1.0 collective-permute-start.28
  90.7 1.9 %collective-permute-start.29 = (f32[16,16,128]{2,1,0:T(8,128)S(1)}, f32[16,16,128]{2,1,0:T(8,128)S(1)}, u32[]{:S(2)}, u32[]{:S(2)}) collective-permute-start(f32[16,16,128]{2,1,0:T(8,128)S(1)} %get-tuple-element.71), channel_id=1, source_target_pairs={{0,24},{8,16},{16,8},{24,0},{1,25},{9,17},{17,9},{25,1},{2,26},{10... | collective-permute-start | bytes 393224 | tf_op jit(solution)/shard_map/ppermute | solution.py:411
  92.7 4.2 %collective-permute-done.11.rest_0_ = f32[16,64,128]{2,1,0:T(8,128)S(1)} collective-permute-done((f32[16,64,128]{2,1,0:T(8,128)S(1)}, f32[16,64,128]{2,1,0:T(8,128)S(1)}, u32[]{:S(2)}, u32[]{:S(2)}) %collective-permute-start.11) | collective-permute-done | bytes 524320 | tf_op jit(solution)/shard_map/ppermute | solution.py:427
  96.9 0.8 collective-permute-start.23
  97.7 3.3 %transport_outer_rows.5 = (f32[17,16,128]{2,1,0:T(8,128)S(1)}, f32[17,16,128]{2,1,0:T(8,128)S(1)}, f32[17,16,128]{2,1,0:T(8,128)S(1)}, f32[17,16,128]{2,1,0:T(8,128)S(1)}) custom-call(s32[1]{0:T(128)} %bitcast.me_ref.refs_0_, s32[1]{0:T(128)} %bitcast.4.odd_ref, f32[16]{0:T(128)S(1)} %copy-done.3, f32[16]{0:T(128)S(1)} %copy-done.4, ...), custom_call_target="tpu_custom_call" | custom-call | flops 5242880 | bytes 2621440 | tf_op jit(solution)/shard_map/transport_outer_rows/pallas_call | solution.py:430
  101.1 3.3 %transport_outer_rows.7 = (f32[16,16,128]{2,1,0:T(8,128)S(1)}, f32[16,16,128]{2,1,0:T(8,128)S(1)}, f32[16,16,128]{2,1,0:T(8,128)S(1)}, f32[16,16,128]{2,1,0:T(8,128)S(1)}) custom-call(s32[1]{0:T(128)} %bitcast.me_ref.refs_0_, s32[1]{0:T(128)} %bitcast.4.odd_ref, f32[16]{0:T(128)S(1)} %copy-done.3, f32[16]{0:T(128)S(1)} %copy-done.4, ...), custom_call_target="tpu_custom_call" | custom-call | flops 5242880 | bytes 2621440 | tf_op jit(solution)/shard_map/transport_outer_rows/pallas_call | solution.py:430
  104.4 0.2 collective-permute-start.4
  104.7 1.1 collective-permute-start.5
  105.8 0.6 collective-permute-start.6
  106.4 1.2 collective-permute-start.24
  107.6 0.2 collective-permute-start.17
  107.7 3.3 %transport_outer_rows.6 = (f32[16,16,128]{2,1,0:T(8,128)S(1)}, f32[16,16,128]{2,1,0:T(8,128)S(1)}, f32[16,16,128]{2,1,0:T(8,128)S(1)}, f32[16,16,128]{2,1,0:T(8,128)S(1)}) custom-call(s32[1]{0:T(128)} %bitcast.me_ref.refs_0_, s32[1]{0:T(128)} %bitcast.4.odd_ref, f32[16]{0:T(128)S(1)} %copy-done.3, f32[16]{0:T(128)S(1)} %copy-done.4, ...), custom_call_target="tpu_custom_call" | custom-call | flops 5242880 | bytes 2621440 | tf_op jit(solution)/shard_map/transport_outer_rows/pallas_call | solution.py:430
  111.0 4.8 %collective-permute-done.24.refs_15_ = f32[16,16,128]{2,1,0:T(8,128)S(1)} collective-permute-done((f32[16,16,128]{2,1,0:T(8,128)S(1)}, f32[16,16,128]{2,1,0:T(8,128)S(1)}, u32[]{:S(2)}, u32[]{:S(2)}) %collective-permute-start.24) | collective-permute-done | bytes 131104 | tf_op jit(solution)/shard_map/ppermute | solution.py:411
  115.8 1.3 collective-permute-start.18
  117.1 0.4 collective-permute-start.19
  117.6 0.4 collective-permute-start.12
  117.9 1.3 collective-permute-start.13
  119.7 3.3 %couple_sections.5 = (f32[64,5,8,512]{3,2,1,0:T(8,128)}, f32[5,8,512]{2,1,0:T(8,128)}, f32[8,64,512]{2,1,0:T(8,128)S(1)}) custom-call(s32[1]{0:T(128)} %bitcast.me_ref.refs_0_, f32[64]{0:T(128)S(1)} %copy-done.5, bf16[64,192]{1,0:T(8,128)(2,1)S(1)} %pad_maximum_fusion.refs_2_, f32[32,128]{1,0:T(8,128)S(1)} %bitcast.21, ...), custom_call_target="tpu_custom_call" | custom-call | flops 33554432 | bytes 3145728 | tf_op jit(solution)/shard_map/couple_sections/pallas_call | solution.py:498
  123.0 3.1 %couple_sections.6 = (f32[64,5,8,512]{3,2,1,0:T(8,128)}, f32[5,8,512]{2,1,0:T(8,128)}) custom-call(s32[1]{0:T(128)} %bitcast.me_ref.refs_0_, f32[64]{0:T(128)S(1)} %copy-done.5, bf16[64,192]{1,0:T(8,128)(2,1)S(1)} %pad_maximum_fusion.refs_2_, f32[32,128]{1,0:T(8,128)S(1)} %bitcast.22, ...), custom_call_target="tpu_custom_call", output_to_operand_aliasing={{0}: (17, {}), {1}: (18, {})} | custom-call | flops 33554432 | bytes 3145728 | tf_op jit(solution)/shard_map/couple_sections/pallas_call | solution.py:498
  126.1 3.1 %couple_sections.7 = (f32[64,5,8,512]{3,2,1,0:T(8,128)}, f32[5,8,512]{2,1,0:T(8,128)}) custom-call(s32[1]{0:T(128)} %bitcast.me_ref.refs_0_, f32[64]{0:T(128)S(1)} %copy-done.5, bf16[64,192]{1,0:T(8,128)(2,1)S(1)} %pad_maximum_fusion.refs_2_, f32[32,128]{1,0:T(8,128)S(1)} %bitcast.23, ...), custom_call_target="tpu_custom_call", output_to_operand_aliasing={{0}: (17, {}), {1}: (18, {})} | custom-call | flops 33554432 | bytes 3145728 | tf_op jit(solution)/shard_map/couple_sections/pallas_call | solution.py:498
  129.1 3.1 %couple_sections.8 = (f32[64,5,8,512]{3,2,1,0:T(8,128)}, f32[5,8,512]{2,1,0:T(8,128)}) custom-call(s32[1]{0:T(128)} %bitcast.me_ref.refs_0_, f32[64]{0:T(128)S(1)} %copy-done.5, bf16[64,192]{1,0:T(8,128)(2,1)S(1)} %pad_maximum_fusion.refs_2_, f32[32,128]{1,0:T(8,128)S(1)} %bitcast.24, ...), custom_call_target="tpu_custom_call", output_to_operand_aliasing={{0}: (17, {}), {1}: (18, {})} | custom-call | flops 33554432 | bytes 3145728 | tf_op jit(solution)/shard_map/couple_sections/pallas_call | solution.py:498
  132.2 3.1 %couple_sections.9 = (f32[64,5,8,512]{3,2,1,0:T(8,128)}, f32[5,8,512]{2,1,0:T(8,128)}) custom-call(s32[1]{0:T(128)} %bitcast.me_ref.refs_0_, f32[64]{0:T(128)S(1)} %copy-done.5, bf16[64,192]{1,0:T(8,128)(2,1)S(1)} %pad_maximum_fusion.refs_2_, f32[32,128]{1,0:T(8,128)S(1)} %bitcast.25, ...), custom_call_target="tpu_custom_call", output_to_operand_aliasing={{0}: (17, {}), {1}: (18, {})} | custom-call | flops 33554432 | bytes 3145728 | tf_op jit(solution)/shard_map/couple_sections/pallas_call | solution.py:498
  (54 shorter events, 0.7 us)
Async XLA Ops:
  0.6 0.8 copy-start
  1.5 0.8 copy-start.1
  2.3 0.7 copy-start.2
  4.7 17.3 %copy-start.9 = (f32[16,5]{0,1:T(8,128)S(1)}, f32[16,5]{0,1:T(8,128)}, u32[]{:S(2)}) copy-start(f32[16,5]{0,1:T(8,128)} %param.13) | copy-start | bytes 964
  4.7 17.4 %copy-start.3 = (f32[16]{0:T(128)S(1)}, f32[16]{0:T(128)}, u32[]{:S(2)}) copy-start(f32[16]{0:T(128)} %ux_ref.15) | copy-start | bytes 196
  4.8 17.3 %copy-start.4 = (f32[16]{0:T(128)S(1)}, f32[16]{0:T(128)}, u32[]{:S(2)}) copy-start(f32[16]{0:T(128)} %uy_ref.11) | copy-start | bytes 196
  4.8 27.2 %collective-permute-start.20 = (f32[16,64,128]{2,1,0:T(8,128)S(1)}, f32[16,64,128]{2,1,0:T(8,128)}, u32[]{:S(2)}, u32[]{:S(2)}) collective-permute-start(f32[16,64,128]{2,1,0:T(8,128)S(1)} %get-tuple-element.62), channel_id=1, source_target_pairs={{2,0},{4,2},{6,4},{1,3},{3,5},{5,7},{10,8},{12,10},{14,12},{9,11},... | collective-permute-start | bytes 1572872 | tf_op jit(solution)/shard_map/ppermute | solution.py:424
  9.1 23.0 %collective-permute-start.25 = (f32[16,64,128]{2,1,0:T(8,128)}, f32[16,64,128]{2,1,0:T(8,128)S(1)}, u32[]{:S(2)}, u32[]{:S(2)}) collective-permute-start(f32[16,64,128]{2,1,0:T(8,128)} %get-tuple-element.67), channel_id=1, source_target_pairs={{0,1},{1,0},{2,3},{3,2},{4,5},{5,4},{6,7},{7,6},{8,9},{9,8},{10,11... | collective-permute-start | bytes 1572872 | tf_op jit(solution)/shard_map/ppermute | solution.py:421
  15.0 20.0 %collective-permute-start.10 = (f32[16,64,128]{2,1,0:T(8,128)S(1)}, f32[16,64,128]{2,1,0:T(8,128)}, u32[]{:S(2)}, u32[]{:S(2)}) collective-permute-start(f32[16,64,128]{2,1,0:T(8,128)S(1)} %get-tuple-element.51), channel_id=1, source_target_pairs={{2,0},{4,2},{6,4},{1,3},{3,5},{5,7},{10,8},{12,10},{14,12},{9,11},... | collective-permute-start | bytes 1572872 | tf_op jit(solution)/shard_map/ppermute | solution.py:424
  16.3 28.1 %collective-permute-start.15 = (f32[16,64,128]{2,1,0:T(8,128)S(1)}, f32[16,64,128]{2,1,0:T(8,128)}, u32[]{:S(2)}, u32[]{:S(2)}) collective-permute-start(f32[16,64,128]{2,1,0:T(8,128)S(1)} %get-tuple-element.57), channel_id=1, source_target_pairs={{2,0},{4,2},{6,4},{1,3},{3,5},{5,7},{10,8},{12,10},{14,12},{9,11},... | collective-permute-start | bytes 1572872 | tf_op jit(solution)/shard_map/ppermute | solution.py:424
  17.6 46.6 %collective-permute-start.2 = (f32[16,64,128]{2,1,0:T(8,128)S(1)}, f32[16,64,128]{2,1,0:T(8,128)S(1)}, u32[]{:S(2)}, u32[]{:S(2)}) collective-permute-start(f32[16,64,128]{2,1,0:T(8,128)S(1)} %get-tuple-element.42), channel_id=1, source_target_pairs={{0,1},{1,0},{2,3},{3,2},{4,5},{5,4},{6,7},{7,6},{8,9},{9,8},{10,11... | collective-permute-start | bytes 1572872 | tf_op jit(solution)/shard_map/ppermute | solution.py:421
  32.0 32.2 %collective-permute-start.7 = (f32[16,80,128]{2,1,0:T(8,128)S(1)}, f32[16,80,128]{2,1,0:T(8,128)S(1)}, u32[]{:S(2)}, u32[]{:S(2)}) collective-permute-start(f32[16,80,128]{2,1,0:T(8,128)S(1)} %get-tuple-element.48), channel_id=1, source_target_pairs={{0,8},{8,0},{16,24},{24,16},{1,9},{9,1},{17,25},{25,17},{2,10},{10... | collective-permute-start | bytes 1966088 | tf_op jit(solution)/shard_map/ppermute | solution.py:411
  32.1 39.3 %collective-permute-start.26 = (f32[16,64,128]{2,1,0:T(8,128)S(1)}, f32[16,64,128]{2,1,0:T(8,128)S(1)}, u32[]{:S(2)}, u32[]{:S(2)}) collective-permute-start(f32[16,64,128]{2,1,0:T(8,128)S(1)} %collective-permute-done.25.rest_0_), channel_id=1, source_target_pairs={{0,2},{2,4},{4,6},{3,1},{5,3},{7,5},{8,10},{10,12},{12,14},{11,9},... | collective-permute-start | bytes 1572872 | tf_op jit(solution)/shard_map/ppermute | solution.py:422
  46.0 25.5 %collective-permute-start.21 = (f32[16,64,128]{2,1,0:T(8,128)S(1)}, f32[16,64,128]{2,1,0:T(8,128)S(1)}, u32[]{:S(2)}, u32[]{:S(2)}) collective-permute-start(f32[16,64,128]{2,1,0:T(8,128)S(1)} %get-tuple-element.86), channel_id=1, source_target_pairs={{0,1},{1,0},{2,3},{3,2},{4,5},{5,4},{6,7},{7,6},{8,9},{9,8},{10,11... | collective-permute-start | bytes 1572872 | tf_op jit(solution)/shard_map/ppermute | solution.py:427
  46.7 13.1 %collective-permute-start.1 = (f32[64,128]{1,0:T(8,128)S(1)}, f32[64,128]{1,0:T(8,128)S(1)}, u32[]{:S(2)}, u32[]{:S(2)}) collective-permute-start(f32[64,128]{1,0:T(8,128)S(1)} %get-tuple-element.80), channel_id=1, source_target_pairs={{1,0},{2,1},{3,2},{4,3},{5,4},{6,5},{7,6},{9,8},{10,9},{11,10},{12... | collective-permute-start | bytes 98312 | tf_op jit(solution)/shard_map/ppermute | solution.py:387
  59.9 3.0 %collective-permute-start = (f32[64,128]{1,0:T(8,128)S(1)}, f32[64,128]{1,0:T(8,128)S(1)}, u32[]{:S(2)}, u32[]{:S(2)}) collective-permute-start(f32[64,128]{1,0:T(8,128)S(1)} %get-tuple-element.81), channel_id=1, source_target_pairs={{0,1},{1,2},{2,3},{3,4},{4,5},{5,6},{6,7},{8,9},{9,10},{10,11},{11... | collective-permute-start | bytes 98312 | tf_op jit(solution)/shard_map/ppermute | solution.py:386
  62.9 17.7 %collective-permute-start.8 = (f32[16,80,128]{2,1,0:T(8,128)S(1)}, f32[16,80,128]{2,1,0:T(8,128)S(1)}, u32[]{:S(2)}, u32[]{:S(2)}) collective-permute-start(f32[16,80,128]{2,1,0:T(8,128)S(1)} %get-tuple-element.49), channel_id=1, source_target_pairs={{0,16},{8,24},{16,0},{24,8},{1,17},{9,25},{17,1},{25,9},{2,18},{10... | collective-permute-start | bytes 1966088 | tf_op jit(solution)/shard_map/ppermute | solution.py:411
  64.2 25.5 %collective-permute-start.9 = (f32[16,80,128]{2,1,0:T(8,128)S(1)}, f32[16,80,128]{2,1,0:T(8,128)S(1)}, u32[]{:S(2)}, u32[]{:S(2)}) collective-permute-start(f32[16,80,128]{2,1,0:T(8,128)S(1)} %get-tuple-element.50), channel_id=1, source_target_pairs={{0,24},{8,16},{16,8},{24,0},{1,25},{9,17},{17,9},{25,1},{2,26},{10... | collective-permute-start | bytes 1966088 | tf_op jit(solution)/shard_map/ppermute | solution.py:411
  64.2 26.5 %collective-permute-start.3 = (f32[16,64,128]{2,1,0:T(8,128)S(1)}, f32[16,64,128]{2,1,0:T(8,128)S(1)}, u32[]{:S(2)}, u32[]{:S(2)}) collective-permute-start(f32[16,64,128]{2,1,0:T(8,128)S(1)} %collective-permute-done.2.rest_0_), channel_id=1, source_target_pairs={{0,2},{2,4},{4,6},{3,1},{5,3},{7,5},{8,10},{10,12},{12,14},{11,9},... | collective-permute-start | bytes 1572872 | tf_op jit(solution)/shard_map/ppermute | solution.py:422
  71.4 21.2 %collective-permute-start.16 = (f32[16,64,128]{2,1,0:T(8,128)S(1)}, f32[16,64,128]{2,1,0:T(8,128)S(1)}, u32[]{:S(2)}, u32[]{:S(2)}) collective-permute-start(f32[16,64,128]{2,1,0:T(8,128)S(1)} %get-tuple-element.87), channel_id=1, source_target_pairs={{0,1},{1,0},{2,3},{3,2},{4,5},{5,4},{6,7},{7,6},{8,9},{9,8},{10,11... | collective-permute-start | bytes 1572872 | tf_op jit(solution)/shard_map/ppermute | solution.py:427
  71.5 25.4 %collective-permute-start.11 = (f32[16,64,128]{2,1,0:T(8,128)S(1)}, f32[16,64,128]{2,1,0:T(8,128)S(1)}, u32[]{:S(2)}, u32[]{:S(2)}) collective-permute-start(f32[16,64,128]{2,1,0:T(8,128)S(1)} %get-tuple-element.88), channel_id=1, source_target_pairs={{0,1},{1,0},{2,3},{3,2},{4,5},{5,4},{6,7},{7,6},{8,9},{9,8},{10,11... | collective-permute-start | bytes 1572872 | tf_op jit(solution)/shard_map/ppermute | solution.py:427
  73.5 24.2 %copy-start.6 = (f32[64,64]{1,0:T(8,128)S(1)}, f32[64,64]{1,0:T(8,128)}, u32[]{:S(2)}) copy-start(f32[64,64]{1,0:T(8,128)} %param.16) | copy-start | bytes 49156
  80.6 23.9 %collective-permute-start.27 = (f32[16,16,128]{2,1,0:T(8,128)S(1)}, f32[16,16,128]{2,1,0:T(8,128)S(1)}, u32[]{:S(2)}, u32[]{:S(2)}) collective-permute-start(f32[16,16,128]{2,1,0:T(8,128)S(1)} %get-tuple-element.69), channel_id=1, source_target_pairs={{0,8},{8,0},{16,24},{24,16},{1,9},{9,1},{17,25},{25,17},{2,10},{10... | collective-permute-start | bytes 393224 | tf_op jit(solution)/shard_map/ppermute | solution.py:411
  89.7 15.0 %collective-permute-start.28 = (f32[16,16,128]{2,1,0:T(8,128)S(1)}, f32[16,16,128]{2,1,0:T(8,128)S(1)}, u32[]{:S(2)}, u32[]{:S(2)}) collective-permute-start(f32[16,16,128]{2,1,0:T(8,128)S(1)} %get-tuple-element.70), channel_id=1, source_target_pairs={{0,16},{8,24},{16,0},{24,8},{1,17},{9,25},{17,1},{25,9},{2,18},{10... | collective-permute-start | bytes 393224 | tf_op jit(solution)/shard_map/ppermute | solution.py:411
  90.7 15.1 %collective-permute-start.29 = (f32[16,16,128]{2,1,0:T(8,128)S(1)}, f32[16,16,128]{2,1,0:T(8,128)S(1)}, u32[]{:S(2)}, u32[]{:S(2)}) collective-permute-start(f32[16,16,128]{2,1,0:T(8,128)S(1)} %get-tuple-element.71), channel_id=1, source_target_pairs={{0,24},{8,16},{16,8},{24,0},{1,25},{9,17},{17,9},{25,1},{2,26},{10... | collective-permute-start | bytes 393224 | tf_op jit(solution)/shard_map/ppermute | solution.py:411
  92.7 13.7 %collective-permute-start.22 = (f32[16,16,128]{2,1,0:T(8,128)S(1)}, f32[16,16,128]{2,1,0:T(8,128)S(1)}, u32[]{:S(2)}, u32[]{:S(2)}) collective-permute-start(f32[16,16,128]{2,1,0:T(8,128)S(1)} %get-tuple-element.64), channel_id=1, source_target_pairs={{0,8},{8,0},{16,24},{24,16},{1,9},{9,1},{17,25},{25,17},{2,10},{10... | collective-permute-start | bytes 393224 | tf_op jit(solution)/shard_map/ppermute | solution.py:411
  96.9 10.6 %collective-permute-start.23 = (f32[16,16,128]{2,1,0:T(8,128)S(1)}, f32[16,16,128]{2,1,0:T(8,128)S(1)}, u32[]{:S(2)}, u32[]{:S(2)}) collective-permute-start(f32[16,16,128]{2,1,0:T(8,128)S(1)} %get-tuple-element.65), channel_id=1, source_target_pairs={{0,16},{8,24},{16,0},{24,8},{1,17},{9,25},{17,1},{25,9},{2,18},{10... | collective-permute-start | bytes 393224 | tf_op jit(solution)/shard_map/ppermute | solution.py:411
  97.7 10.0 %copy-start.7 = (f32[64,64]{1,0:T(8,128)S(1)}, f32[64,64]{1,0:T(8,128)}, u32[]{:S(2)}) copy-start(f32[64,64]{1,0:T(8,128)} %param.17) | copy-start | bytes 49156
  101.1 18.4 %copy-start.8 = (f32[8,512]{1,0:T(8,128)S(1)}, f32[8,512]{1,0:T(8,128)}, u32[]{:S(2)}) copy-start(f32[8,512]{1,0:T(8,128)} %param.19) | copy-start | bytes 49156
  101.1 18.5 %copy-start.5 = (f32[64]{0:T(128)S(1)}, f32[64]{0:T(128)}, u32[]{:S(2)}) copy-start(f32[64]{0:T(128)} %refs_1_.9) | copy-start | bytes 772
  104.4 13.2 %collective-permute-start.4 = (f32[17,16,128]{2,1,0:T(8,128)S(1)}, f32[17,16,128]{2,1,0:T(8,128)S(1)}, u32[]{:S(2)}, u32[]{:S(2)}) collective-permute-start(f32[17,16,128]{2,1,0:T(8,128)S(1)} %get-tuple-element.44), channel_id=1, source_target_pairs={{0,8},{8,0},{16,24},{24,16},{1,9},{9,1},{17,25},{25,17},{2,10},{10... | collective-permute-start | bytes 417800 | tf_op jit(solution)/shard_map/ppermute | solution.py:411
  104.7 13.3 %collective-permute-start.5 = (f32[17,16,128]{2,1,0:T(8,128)S(1)}, f32[17,16,128]{2,1,0:T(8,128)S(1)}, u32[]{:S(2)}, u32[]{:S(2)}) collective-permute-start(f32[17,16,128]{2,1,0:T(8,128)S(1)} %get-tuple-element.45), channel_id=1, source_target_pairs={{0,16},{8,24},{16,0},{24,8},{1,17},{9,25},{17,1},{25,9},{2,18},{10... | collective-permute-start | bytes 417800 | tf_op jit(solution)/shard_map/ppermute | solution.py:411
  105.8 13.5 %collective-permute-start.6 = (f32[17,16,128]{2,1,0:T(8,128)S(1)}, f32[17,16,128]{2,1,0:T(8,128)S(1)}, u32[]{:S(2)}, u32[]{:S(2)}) collective-permute-start(f32[17,16,128]{2,1,0:T(8,128)S(1)} %get-tuple-element.46), channel_id=1, source_target_pairs={{0,24},{8,16},{16,8},{24,0},{1,25},{9,17},{17,9},{25,1},{2,26},{10... | collective-permute-start | bytes 417800 | tf_op jit(solution)/shard_map/ppermute | solution.py:411
  106.4 9.4 %collective-permute-start.24 = (f32[16,16,128]{2,1,0:T(8,128)S(1)}, f32[16,16,128]{2,1,0:T(8,128)S(1)}, u32[]{:S(2)}, u32[]{:S(2)}) collective-permute-start(f32[16,16,128]{2,1,0:T(8,128)S(1)} %get-tuple-element.66), channel_id=1, source_target_pairs={{0,24},{8,16},{16,8},{24,0},{1,25},{9,17},{17,9},{25,1},{2,26},{10... | collective-permute-start | bytes 393224 | tf_op jit(solution)/shard_map/ppermute | solution.py:411
  107.6 9.6 %collective-permute-start.17 = (f32[16,16,128]{2,1,0:T(8,128)S(1)}, f32[16,16,128]{2,1,0:T(8,128)S(1)}, u32[]{:S(2)}, u32[]{:S(2)}) collective-permute-start(f32[16,16,128]{2,1,0:T(8,128)S(1)} %get-tuple-element.59), channel_id=1, source_target_pairs={{0,8},{8,0},{16,24},{24,16},{1,9},{9,1},{17,25},{25,17},{2,10},{10... | collective-permute-start | bytes 393224 | tf_op jit(solution)/shard_map/ppermute | solution.py:411
  115.8 13.3 %collective-permute-start.18 = (f32[16,16,128]{2,1,0:T(8,128)S(1)}, f32[16,16,128]{2,1,0:T(8,128)S(1)}, u32[]{:S(2)}, u32[]{:S(2)}) collective-permute-start(f32[16,16,128]{2,1,0:T(8,128)S(1)} %get-tuple-element.60), channel_id=1, source_target_pairs={{0,16},{8,24},{16,0},{24,8},{1,17},{9,25},{17,1},{25,9},{2,18},{10... | collective-permute-start | bytes 393224 | tf_op jit(solution)/shard_map/ppermute | solution.py:411
  117.1 12.0 %collective-permute-start.19 = (f32[16,16,128]{2,1,0:T(8,128)S(1)}, f32[16,16,128]{2,1,0:T(8,128)S(1)}, u32[]{:S(2)}, u32[]{:S(2)}) collective-permute-start(f32[16,16,128]{2,1,0:T(8,128)S(1)} %get-tuple-element.61), channel_id=1, source_target_pairs={{0,24},{8,16},{16,8},{24,0},{1,25},{9,17},{17,9},{25,1},{2,26},{10... | collective-permute-start | bytes 393224 | tf_op jit(solution)/shard_map/ppermute | solution.py:411
  117.6 14.6 %collective-permute-start.12 = (f32[16,16,128]{2,1,0:T(8,128)S(1)}, f32[16,16,128]{2,1,0:T(8,128)S(1)}, u32[]{:S(2)}, u32[]{:S(2)}) collective-permute-start(f32[16,16,128]{2,1,0:T(8,128)S(1)} %get-tuple-element.53), channel_id=1, source_target_pairs={{0,8},{8,0},{16,24},{24,16},{1,9},{9,1},{17,25},{25,17},{2,10},{10... | collective-permute-start | bytes 393224 | tf_op jit(solution)/shard_map/ppermute | solution.py:411
  117.9 14.3 %collective-permute-start.13 = (f32[16,16,128]{2,1,0:T(8,128)S(1)}, f32[16,16,128]{2,1,0:T(8,128)S(1)}, u32[]{:S(2)}, u32[]{:S(2)}) collective-permute-start(f32[16,16,128]{2,1,0:T(8,128)S(1)} %get-tuple-element.54), channel_id=1, source_target_pairs={{0,16},{8,24},{16,0},{24,8},{1,17},{9,25},{17,1},{25,9},{2,18},{10... | collective-permute-start | bytes 393224 | tf_op jit(solution)/shard_map/ppermute | solution.py:411
  119.3 12.9 %collective-permute-start.14 = (f32[16,16,128]{2,1,0:T(8,128)S(1)}, f32[16,16,128]{2,1,0:T(8,128)S(1)}, u32[]{:S(2)}, u32[]{:S(2)}) collective-permute-start(f32[16,16,128]{2,1,0:T(8,128)S(1)} %get-tuple-element.55), channel_id=1, source_target_pairs={{0,24},{8,16},{16,8},{24,0},{1,25},{9,17},{17,9},{25,1},{2,26},{10... | collective-permute-start | bytes 393224 | tf_op jit(solution)/shard_map/ppermute | solution.py:411
where the time goes:
time: 136 us; the launch traced here: 135 us
  Pallas kernels  46.6 us (34%)
  starting transfers between devices  42 us (31%)
  waiting for transfers between devices  41.4 us (30%)
  local copies, waits for them, and re-layouts  2.47 us (2%)
  other arithmetic  1.84 us (1%)
    pallas_call x5, Pallas kernels, shards(): pl.pallas_call(functools.partial(outer_kernel, moment, len(halos), blocks...  16.5 us
    pallas_call x5, Pallas kernels, shards(): pl.pallas_call(functools.partial(couple_kernel, first, groups, group_size...  15.7 us
    ppermute x18, waiting for transfers between devices, exchange(): lax.ppermute(parts[k], 'sec', [(i, i ^ k) for i in range(groups)])  14.4 us
    ppermute x18, starting transfers between devices, exchange(): lax.ppermute(parts[k], 'sec', [(i, i ^ k) for i in range(groups)])  12.1 us
    ppermute x1, waiting for transfers between devices, shards(): lax.ppermute(code[:edge], 'space', [(i + 1, i) for i in range(slabs - 1)])  11.9 us
    ppermute x2, starting transfers between devices, shards(): near = lax.ppermute(chosen[moment], 'space', swap)  10.3 us
    ppermute x2, starting transfers between devices, shards(): halos = [near, lax.ppermute(near, 'space', outward)]  10.1 us
    pallas_call x1, Pallas kernels, shards(): pl.pallas_call(functools.partial(inner_kernel, moments, blocks, TOGETHER_...  9.85 us
  transfers between devices with their start and end apart: 30, of which 7 were waited for; matrix products, arithmetic and copies ran while one was open for 1% of the time, Pallas kernels for 31%

commit v1 on v0

v1 whole, which is shorter than its diff:
```python
import functools

import jax
import jax.numpy as jnp
from jax import lax
from jax.experimental import pallas as pl
from jax.experimental.pallas import tpu as pltpu
from jax.sharding import PartitionSpec as P

SUB = 4
ROWS = 2 * SUB
LANES = 128
TILE = 8
F32 = jnp.float32
BF16 = jnp.bfloat16
TOGETHER_INNER = 5
TOGETHER_OUTER = 4
VMEM_LIMIT = 48 * 1024 * 1024


def stacked(array):
    *lead, rows, columns = array.shape
    tiles = columns // LANES
    array = array.reshape(*lead, rows, tiles, LANES)
    return jnp.swapaxes(array, -3, -2).reshape(*lead, rows * tiles, LANES)


def sublane(shape=(TILE, LANES)):
    return lax.broadcasted_iota(jnp.int32, shape, 0)


class Wind:
    def __init__(self, speed_x, speed_y, blocks):
        self.a, self.b = jnp.abs(speed_x), jnp.abs(speed_y)
        self.own = 1.0 - self.a - self.b
        self.blocks = blocks
        self.positive_x = speed_x > 0.0
        self.positive_y = speed_y > 0.0
        lane = lax.broadcasted_iota(jnp.int32, (TILE, LANES), 1)
        self.lane_shift = jnp.where(self.positive_y, 1, LANES - 1).astype(jnp.int32)
        self.band_shift = jnp.where(self.positive_y, 1, TILE - 1).astype(jnp.int32)
        self.edge = lane == jnp.where(self.positive_y, 0, LANES - 1)
        self.border = sublane() == jnp.where(self.positive_y, 0, TILE - 1)

    def row(self, u, first, last):
        return jnp.where(self.positive_x, first + u, last - u)

    def block(self, j):
        return jnp.where(self.positive_y, j, self.blocks - 1 - j)


def substeps(chains):
    states = [chain[1] for chain in chains]
    for step in range(1, SUB + 1):
        fresh = []
        for (wind, _, code, value), state in zip(chains, states):
            rows = [None] * step
            for u in range(step, ROWS):
                turned = [pltpu.roll(tile, wind.lane_shift, axis=1) for tile in state[u]]
                wrap = pltpu.roll(turned[-1], wind.band_shift, axis=0)
                behind = [jnp.where(wind.border, 0.0, wrap)] + turned[:-1]
                tiles = []
                for j, tile in enumerate(state[u]):
                    side = jnp.where(wind.edge, behind[j], turned[j])
                    moved = wind.own * tile + wind.a * state[u - 1][j] + wind.b * side
                    kind = code(u, j)
                    tiles.append(jnp.where(kind < 0.0, moved, kind * value))
                rows.append(tiles)
            fresh.append(rows)
        states = fresh
    return states


def keep(wind, state, packed):
    blocks = wind.blocks
    for u in range(SUB, ROWS):
        row = wind.row(u, -SUB, ROWS - 1)
        for j, tile in enumerate(state[u]):
            packed[pl.ds(row * blocks + wind.block(j), TILE, stride=SUB * blocks), :] = tile


def scatter(packed, me, outs):
    share = packed.shape[0] // len(outs)
    for k, (out, spot) in enumerate(outs):
        start = pl.multiple_of((me ^ k) * share, share)
        out[spot] = packed[pl.ds(start, share), :]


def select_kernel(outs, blocks, ux_ref, *refs):
    count = sum(outs)
    x_refs, refs = refs[:count], refs[count:]
    coded = len(refs) > len(outs) + 1
    if coded:
        wall_hbm, inflow_hbm, *refs, wall_ref, inflow_ref, sems = refs
        refs = [None] + refs
    out_refs = refs[1 : 1 + len(outs)]
    per_step = x_refs[0].shape[0]
    step = pl.program_id(0)
    spacing = blocks * ROWS
    edge = SUB * blocks * TILE

    def loads():
        return (
            pltpu.make_async_copy(wall_hbm, wall_ref, sems.at[0]),
            pltpu.make_async_copy(inflow_hbm, inflow_ref, sems.at[1]),
        )

    if coded:

        @pl.when(step == 0)
        def _():
            for load in loads():
                load.start()

    def section(s, carry):
        number = step * per_step + s
        first = jnp.where(ux_ref[number] > 0.0, SUB, 0)
        sources = iter(x_refs)
        for held, out_ref in zip(outs, out_refs):
            for i in range(held):
                x_ref = next(sources)
                for row in range(SUB):
                    for block in range(blocks):
                        spot = i * edge + (row * blocks + block) * TILE
                        out_ref[number, spot : spot + TILE, :] = x_ref[
                            s, pl.ds(block * ROWS + first + row, TILE, stride=spacing), :
                        ]
        return carry

    lax.fori_loop(0, per_step, section, 0, unroll=2)
    if coded:
        code_ref = refs[-1]

        @pl.when(step == pl.num_programs(0) - 1)
        def _():
            for load in loads():
                load.wait()
            last = out_refs[0].shape[0] - 2
            for row in range(ROWS):
                for block in range(blocks):
                    spot = (row * blocks + block) * TILE
                    source = pl.ds(block * ROWS + row, TILE, stride=spacing)
                    inflow = jnp.where(inflow_ref[source, :] > 0, 1.0, -1.0)
                    kind = jnp.where(wall_ref[source, :] > 0, 0.0, inflow)
                    code_ref[spot : spot + TILE, :] = kind
                    spot -= edge * (row // SUB)
                    out_refs[0][last + row // SUB, spot : spot + TILE, :] = kind


def relay_kernel(moments, odd_ref, ux_ref, _, own_ref, far_ref, *out_refs):
    odd = odd_ref[0]
    sections, size = own_ref.shape[0], own_ref.shape[1] // moments

    def section(s, carry):
        def copy(source):
            for i, out_ref in enumerate(out_refs):
                out_ref[s] = source[s, i * size : (i + 1) * size, :]

        stays = (ux_ref[s] > 0.0) != (odd == 1)
        pl.when(stays)(lambda: copy(own_ref))
        pl.when(jnp.logical_not(stays))(lambda: copy(far_ref))
        return carry

    lax.fori_loop(0, sections, section, 0)


def inner_kernel(
    base, moments, blocks, together, me_ref, ux_ref, uy_ref, inflow_ref, _, code_ref, *rest
):
    x_refs, out_refs, packed = rest[:moments], rest[moments:-1], rest[-1]
    per_step = x_refs[0].shape[0]
    step = pl.program_id(0)
    me = me_ref[0]
    spacing = blocks * ROWS
    share = out_refs[0].shape[1] // moments

    def section(s, carry):
        number = step * per_step + s
        wind = Wind(ux_ref[number], uy_ref[number], blocks)

        def code(u, j):
            spot = (wind.row(u, 0, ROWS - 1) * blocks + wind.block(j)) * TILE
            return code_ref[pl.ds(pl.multiple_of(spot, TILE), TILE), :]

        for low in range(0, moments, together):
            some = range(low, min(moments, low + together))
            chains = []
            for m in some:
                tiles = [
                    [
                        x_refs[m][
                            s,
                            pl.ds(
                                wind.block(j) * ROWS + wind.row(u, 0, ROWS - 1),
                                TILE,
                                stride=spacing,
                            ),
                            :,
                        ]
                        for j in range(blocks)
                    ]
                    for u in range(ROWS)
                ]
                chains.append((wind, tiles, code, inflow_ref[number, base + m]))
            for m, state in zip(some, substeps(chains)):
                keep(wind, state, packed.at[m])
        for m in range(moments):
            scatter(
                packed.at[m],
                me,
                [(out, (s, slice(m * share, (m + 1) * share))) for out in out_refs],
            )
        return carry

    lax.fori_loop(0, per_step, section, 0)


def outer_kernel(
    some, halos, blocks, together, me_ref, odd_ref, ux_ref, uy_ref, inflow_ref, _,
    near_ref, far_ref, code_ref, *rest
):
    count = len(some)
    x_refs, rest = rest[:count], rest[count:]
    halo_refs, rest = rest[: sum(halos)], rest[sum(halos) :]
    out_refs, (codes, packed) = rest[:-2], rest[-2:]
    per_step = x_refs[0].shape[0]
    step = pl.program_id(0)
    me = me_ref[0]
    odd = odd_ref[0]
    spacing = blocks * ROWS
    edge = SUB * blocks * TILE
    share = packed.shape[1] // len(out_refs)

    @pl.when(odd == 1)
    def _():
        codes[:edge] = near_ref[1]
        codes[edge : 2 * edge] = far_ref[0]

    @pl.when(odd != 1)
    def _():
        codes[:edge] = far_ref[1]
        codes[edge : 2 * edge] = near_ref[0]

    codes[2 * edge :] = code_ref[...]

    def sections(turn, carry):
        for m in range(count):
            chains = []
            for i in range(together):
                s = turn * together + i
                number = step * per_step + s
                wind = Wind(ux_ref[number], uy_ref[number], blocks)
                outside = jnp.where(wind.positive_x, 0, edge)
                second = jnp.logical_xor(wind.positive_x, odd == 1)
                first_halo = sum(halos[:m])

                def code(u, j, wind=wind, outside=outside):
                    if u < SUB:
                        spot = outside + (wind.row(u, 0, SUB - 1) * blocks + wind.block(j)) * TILE
                    else:
                        row = wind.row(u, -SUB, ROWS + SUB - 1)
                        spot = 2 * edge + (row * blocks + wind.block(j)) * TILE
                    return codes[pl.ds(pl.multiple_of(spot, TILE), TILE), :]

                tiles = []
                for u in range(ROWS):
                    row = []
                    for j in range(blocks):
                        if u < SUB:
                            spot = (wind.row(u, 0, SUB - 1) * blocks + wind.block(j)) * TILE
                            spot = pl.ds(pl.multiple_of(spot, TILE), TILE)
                            tile = halo_refs[first_halo][s, spot, :]
                            if halos[m] == 2:
                                tile = jnp.where(second, halo_refs[first_halo + 1][s, spot, :], tile)
                        else:
                            start = wind.block(j) * ROWS + wind.row(u, -SUB, ROWS + SUB - 1)
                            tile = x_refs[m][s, pl.ds(start, TILE, stride=spacing), :]
                        row.append(tile)
                    tiles.append(row)
                chains.append((wind, tiles, code, inflow_ref[number, some[m]]))
            for i, (chain, state) in enumerate(zip(chains, substeps(chains))):
                keep(chain[0], state, packed.at[m * together + i])
            for i in range(together):
                number = step * per_step + turn * together + i
                spot = (number, slice(m * share, (m + 1) * share))
                scatter(packed.at[m * together + i], me, [(out, spot) for out in out_refs])
        return carry

    lax.fori_loop(0, per_step // together, sections, 0)
    if some[0] == 0:

        @pl.when(step == 0)
        def _():
            size = out_refs[0].shape[1]
            for number in range(size):
                line = jnp.full((1, LANES), ux_ref[number], F32)
                for out in out_refs:
                    out[size, number : number + 1, :] = line


def split_dot(weights, values):
    high = values.astype(BF16)
    rest = (values - high.astype(F32)).astype(BF16)
    return jnp.dot(
        weights, jnp.concatenate([high, rest, high], axis=0), preferred_element_type=F32
    )


def couple_kernel(first, groups, group_size, blocks, *refs):
    me_ref, rate_ref, share_ref, thermal_ref = refs[:4]
    refs = refs[4:]
    sign_refs, inner, outer = refs[:groups], refs[groups : 2 * groups], refs[2 * groups : 3 * groups]
    refs = refs[3 * groups :]
    if first:
        kernel_ref, spray_ref, gas_ref, merge_ref, *scratch = refs
    else:
        merge_ref, _, _, _, spray_ref, gas_ref, *scratch = refs
    rest, made, total = scratch
    me = me_ref[0]
    sections = groups * group_size
    size = ROWS * blocks
    half = size // 2
    thermal = [thermal_ref[:half, :], thermal_ref[half:, :]]
    gas = tuple(jnp.zeros((half, LANES), F32) for _ in thermal)
    for k in range(groups):

        def section(s, sums, k=k):
            number = (me ^ k) * group_size + s
            flip = jnp.broadcast_to(sign_refs[k][0, pl.ds(s, 1), :], (half, LANES)) > 0.0
            rate = rate_ref[number]
            one, two = inner[k][s], outer[k][s]
            result = []
            for i, moved in enumerate((jnp.where(flip, two, one), jnp.where(flip, one, two))):
                evaporated = (rate * thermal[i]) * moved
                result.append(sums[i] + evaporated)
                rest[pl.ds(pl.multiple_of(number * size + i * half, half), half), :] = moved - evaporated
            return tuple(result)

        gas = lax.fori_loop(0, group_size, section, gas, unroll=4)
    for i in range(2):
        total[i * half : (i + 1) * half, :] = gas[i]
    for block in range(blocks):
        gas_ref[0, :, block * LANES : (block + 1) * LANES] = total[pl.ds(block, ROWS, stride=blocks), :]
    for row in range(ROWS):
        spots = [pl.ds(row * blocks + block, sections, stride=size) for block in range(blocks)]
        cells = jnp.concatenate([rest[spot, :] for spot in spots], axis=1)
        if first:
            merge = split_dot(kernel_ref[...], cells)
            merge_ref[row] = merge
        else:
            merge = merge_ref[row]
        flux = cells * merge
        result = cells - flux + split_dot(share_ref[...], flux)
        for block, spot in enumerate(spots):
            made[spot, :] = result[:, block * LANES : (block + 1) * LANES]

    def write(s, carry):
        for block in range(blocks):
            spray_ref[s, 0, :, block * LANES : (block + 1) * LANES] = made[
                pl.ds(s * size + block, ROWS, stride=blocks), :
            ]
        return carry

    lax.fori_loop(0, sections, write, 0, unroll=8)


def params(**more):
    return pltpu.CompilerParams(vmem_limit_bytes=VMEM_LIMIT, **more)


def split_weights(weights):
    high = lax.reduce_precision(weights, 8, 7)
    return jnp.concatenate([high, high, weights - high], axis=1).astype(BF16)


def shards(
    droplet_integrals,
    flow_number_lengthwise,
    flow_number_crosswise,
    inflow_boundary_integrals,
    boundary_wall_indicator,
    inflow_indicator,
    collision_coefficient,
    collision_target_share,
    evaporation_speed_stepwise,
    thermal_factor,
):
    x, ux, uy = droplet_integrals, flow_number_lengthwise, flow_number_crosswise
    group_size, moments, rows, columns = x.shape
    groups = lax.axis_size("sec")
    slabs = lax.axis_size("space")
    sections = groups * group_size
    width = columns // groups
    blocks = columns // (TILE * LANES)
    size = columns // LANES * ROWS
    share_size = size // 2 // groups
    assert rows == ROWS and slabs % 2 == 0 and TILE % groups == 0

    me = lax.axis_index("sec").astype(jnp.int32).reshape(1)
    odd = (lax.axis_index("space") % 2).astype(jnp.int32).reshape(1)

    swap = [(i, i ^ 1) for i in range(slabs)]
    outward = [(i, i + 2) for i in range(0, slabs - 2, 2)] + [(i, i - 2) for i in range(3, slabs, 2)]
    inward = [(j, i) for i, j in outward]

    smem = pl.BlockSpec(memory_space=pltpu.SMEM)
    anywhere = pl.BlockSpec(memory_space=pl.ANY)
    cells = stacked(x).reshape(group_size, moments * size, LANES)

    def moment_specs(per_step, some):
        return [
            pl.BlockSpec((per_step, size, LANES), lambda g, moment=moment: (g, moment, 0))
            for moment in some
        ]

    def exchange(parts):
        return [parts[0]] + [
            lax.ppermute(parts[k], "sec", [(i, i ^ k) for i in range(groups)])
            for k in range(1, groups)
        ]

    edge = SUB * blocks * TILE
    flat = pl.BlockSpec((size, LANES), lambda g: (0, 0))

    def after(value, *events):
        return lax.optimization_barrier((value, *events))[0]

    def select(outs, last):
        some = sum(outs, ())
        coded = last is None
        per_step = group_size // 2
        operands = [ux] + [cells] * len(some)
        out_shape = [
            jax.ShapeDtypeStruct((group_size + 2 * (held[0] == 0), len(held) * edge, LANES), F32)
            for held in outs
        ]
        out_specs = [pl.BlockSpec(shape.shape, lambda g: (0, 0, 0)) for shape in out_shape]
        scratch = []
        if coded:
            in_specs = [pl.BlockSpec(memory_space=pltpu.HBM)] * 2
            operands += [stacked(boundary_wall_indicator), stacked(inflow_indicator)]
            out_specs.append(flat)
            out_shape.append(jax.ShapeDtypeStruct((size, LANES), F32))
            scratch = [pltpu.VMEM((size, LANES), jnp.int32)] * 2 + [pltpu.SemaphoreType.DMA((2,))]
        else:
            in_specs = [anywhere]
            operands += [last]
        return pl.pallas_call(
            functools.partial(select_kernel, tuple(len(held) for held in outs), blocks),
            grid=(group_size // per_step,),
            in_specs=[smem] + moment_specs(per_step, some) + in_specs,
            out_specs=out_specs,
            out_shape=out_shape,
            scratch_shapes=scratch,
            compiler_params=params(),
            cost_estimate=pl.CostEstimate(
                flops=x.size, bytes_accessed=x.size * 6 * len(some) // moments, transcendentals=0
            ),
            name="select_upwind_rows",
        )(*operands)

    def transport_inner(some, last):
        per_step = 4
        count = len(some)
        return pl.pallas_call(
            functools.partial(inner_kernel, some[0], count, blocks, TOGETHER_INNER),
            grid=(group_size // per_step,),
            in_specs=[smem] * 4 + [anywhere, flat] + moment_specs(per_step, some),
            out_specs=[pl.BlockSpec((per_step, count * share_size, LANES), lambda g: (g, 0, 0))]
            * groups,
            out_shape=[jax.ShapeDtypeStruct((group_size, count * share_size, LANES), F32)] * groups,
            scratch_shapes=[pltpu.VMEM((count, size // 2, LANES), F32)],
            compiler_params=params(),
            cost_estimate=pl.CostEstimate(
                flops=x.size * 4 * count, bytes_accessed=x.size * count, transcendentals=0
            ),
            name="transport_inner_rows",
        )(me, ux, uy, inflow_boundary_integrals, last, code, *[cells] * count)

    def transport_outer(some, halos, last):
        per_step = group_size // 2
        count = len(some)
        length = group_size + (some[0] == 0)
        line = pl.BlockSpec((2, edge, LANES), lambda g: (group_size // 2, 0, 0))
        flat_halos = sum(halos, ())
        return pl.pallas_call(
            functools.partial(
                outer_kernel, some, tuple(len(h) for h in halos), blocks, TOGETHER_OUTER
            ),
            grid=(group_size // per_step,),
            in_specs=[smem] * 5
            + [anywhere, line, line, flat]
            + moment_specs(per_step, some)
            + [pl.BlockSpec((per_step, edge, LANES), lambda g: (g, 0, 0))] * len(flat_halos),
            out_specs=[pl.BlockSpec((length, count * share_size, LANES), lambda g: (0, 0, 0))]
            * groups,
            out_shape=[jax.ShapeDtypeStruct((length, count * share_size, LANES), F32)] * groups,
            scratch_shapes=[
                pltpu.VMEM((2 * edge + size, LANES), F32),
                pltpu.VMEM((count * TOGETHER_OUTER, size // 2, LANES), F32),
            ],
            compiler_params=params(),
            cost_estimate=pl.CostEstimate(
                flops=x.size * 4 * count, bytes_accessed=x.size * 2 * count, transcendentals=0
            ),
            name="transport_outer_rows",
        )(
            me, odd, ux, uy, inflow_boundary_integrals, last, *code_halos, code,
            *[cells] * count, *flat_halos
        )

    def relay(own, far, count, last):
        return pl.pallas_call(
            functools.partial(relay_kernel, count),
            grid=(1,),
            in_specs=[smem, smem, anywhere]
            + [pl.BlockSpec(own.shape, lambda g: (0, 0, 0))] * 2,
            out_specs=[pl.BlockSpec((group_size, edge, LANES), lambda g: (0, 0, 0))] * count,
            out_shape=[jax.ShapeDtypeStruct((group_size, edge, LANES), F32)] * count,
            compiler_params=params(),
            cost_estimate=pl.CostEstimate(
                flops=0, bytes_accessed=own.size * 12, transcendentals=0
            ),
            name="relay_upwind_rows",
        )(odd, ux, last, own, far)

    def swapped(array):
        return lax.ppermute(array, "space", swap)

    def hopped(array, pairs):
        return lax.ppermute(array, "space", pairs)

    chosen_0, chosen_34, code = select([(0,), (3, 4)], None)
    near_0 = swapped(chosen_0)
    far_34 = hopped(chosen_34, inward)
    inner_a = transport_inner((0, 1), chosen_0)
    chosen_1, chosen_2 = select([(1,), (2,)], inner_a[0])
    near_1 = swapped(chosen_1)
    far_0 = hopped(near_0, outward)
    code_halos = (near_0, far_0)
    inner_b = transport_inner((2, 3, 4), chosen_1)
    sent_a = exchange(inner_a)
    near_2 = swapped(after(chosen_2, near_0))
    far_1 = hopped(near_1, outward)
    relayed_3, relayed_4 = relay(chosen_34, far_34, 2, inner_b[0])
    near_3 = swapped(after(relayed_3, near_1))
    far_2 = hopped(near_2, outward)
    near_4 = swapped(after(relayed_4, near_2))
    sent_b = exchange([after(part, *sent_a) for part in inner_b])
    outer_0 = transport_outer((0,), ((near_0, far_0),), after(relayed_3, *sent_a))
    sent_0 = exchange([after(part, *sent_b) for part in outer_0])
    outer_1 = transport_outer((1,), ((near_1, far_1),), after(outer_0[0], *sent_b))
    sent_1 = exchange([after(part, *sent_0) for part in outer_1])
    outer_23 = transport_outer(
        (2, 3), ((near_2, far_2), (near_3,)), after(outer_1[0], *sent_0)
    )
    sent_23 = exchange([after(part, *sent_1) for part in outer_23])
    outer_4 = transport_outer((4,), ((near_4,),), after(outer_23[0], *sent_1))
    sent_4 = exchange(outer_4)
    plan = (
        ((0,), sent_a, 0, sent_0, outer_1[0]),
        ((1,), sent_a, 1, sent_1, outer_23[0]),
        ((2, 3), sent_b, 0, sent_23, outer_4[0]),
        ((4,), sent_b, 2, sent_4, outer_4[0]),
    )

    share = split_weights(collision_target_share)
    kernel = split_weights(collision_coefficient)
    step_width = blocks * LANES
    steps = width // step_width
    step_size = ROWS * blocks
    thermal = thermal_factor.reshape(ROWS, steps, blocks, LANES).swapaxes(0, 1)
    thermal = thermal.reshape(steps * step_size, LANES)
    spray_type = jax.ShapeDtypeStruct((sections, moments, rows, width), F32)
    gas_type = jax.ShapeDtypeStruct((moments, rows, width), F32)
    merge_type = jax.ShapeDtypeStruct((rows, sections, width), F32)
    merge_spec = pl.BlockSpec((rows, sections, step_width), lambda m, j: (0, 0, j))
    spray = gas = merge = None
    for some, inner, base, outer, last in plan:
        first = some[0] == 0

        def part(lead, length, offset):
            return pl.BlockSpec(
                (lead, length, LANES), lambda m, j, offset=offset: (0, (offset + m) * steps + j, 0)
            )

        in_specs = (
            [smem] * 2
            + [
                pl.BlockSpec(share.shape, lambda m, j: (0, 0)),
                pl.BlockSpec((step_size, LANES), lambda m, j: (j, 0)),
            ]
            + [pl.BlockSpec((1, share_size, LANES), lambda m, j: (group_size, 0, 0))] * groups
            + [part(group_size, step_size // 2, base)] * groups
            + [part(group_size, step_size // 2, 0)] * groups
        )
        operands = [me, evaporation_speed_stepwise, share, thermal]
        operands += list(sent_0) + list(inner) + list(outer)
        out_specs = [
            pl.BlockSpec(
                (sections, 1, rows, step_width), lambda m, j, some=some: (0, some[0] + m, 0, j)
            ),
            pl.BlockSpec((1, rows, step_width), lambda m, j, some=some: (some[0] + m, 0, j)),
        ]
        out_shape = [spray_type, gas_type]
        aliases = {}
        if first:
            in_specs.append(pl.BlockSpec(kernel.shape, lambda m, j: (0, 0)))
            operands.append(kernel)
            out_specs.append(merge_spec)
            out_shape.append(merge_type)
        else:
            aliases = {len(operands) + 1: 0, len(operands) + 2: 1}
            in_specs += [merge_spec, anywhere, anywhere, anywhere]
            operands += [merge, spray, gas, last]
        made = pl.pallas_call(
            functools.partial(couple_kernel, first, groups, group_size, blocks),
            grid=(len(some), steps),
            in_specs=in_specs,
            out_specs=out_specs,
            out_shape=out_shape,
            input_output_aliases=aliases,
            scratch_shapes=[pltpu.VMEM((sections * step_size, LANES), F32)] * 2
            + [pltpu.VMEM((step_size, LANES), F32)],
            compiler_params=params(),
            cost_estimate=pl.CostEstimate(
                flops=sections * rows * width * sections * 2 * len(some),
                bytes_accessed=sections * rows * width * 12 * len(some),
                transcendentals=0,
            ),
            name="couple_sections",
        )(*operands)
        if first:
            spray, gas, merge = made
        else:
            spray, gas = made
    return spray, gas


def solution(mesh):
    return jax.shard_map(
        shards,
        mesh=mesh,
        in_specs=(
            P("sec", None, "space", None),
            P("sec"),
            P("sec"),
            P("sec", None),
            P("space", None),
            P("space", None),
            P(),
            P(),
            P(),
            P("space", "sec"),
        ),
        out_specs=(P(None, None, "space", "sec"), P(None, "space", "sec")),
        check_vma=False,
    )
```

time: 136 us -> 110 us (0.81)
  waiting for transfers between devices: 41.4 us -> 19.5 us
  starting transfers between devices: 42 us -> 32 us
  Pallas kernels: 46.6 us -> 52.6 us
  other arithmetic: 1.84 us -> 0.18 us
  local copies, waits for them, and re-layouts: 2.47 us -> 3.9 us
    ppermute x12 -> x9, waiting for transfers between devices: 27 us -> 6.32 us  [the longest x5 6.31 us: swapped(): return lax.ppermute(array, 'space', swap)]
    ppermute x12 -> x9, starting transfers between devices: 30 us -> 21.5 us  [the longest x4 14.4 us: hopped(): return lax.ppermute(array, 'space', pairs)]
    pallas_call x8 -> x9, Pallas kernels: 31 us -> 38 us  [the longest x2 15.5 us: transport_inner(): pl.pallas_call(functools.partial(inner_kernel, some[0], count, blocks, TO...]
    select_n x1 -> x0, other arithmetic: 1.65 us -> none  [shards(): relayed = jnp.where(stays[:, None, None], chosen[moment], far)]
    ppermute x18, starting transfers between devices: 12.1 us -> 10.6 us  [exchange(): lax.ppermute(parts[k], 'sec', [(i, i ^ k) for i in range(groups)])]
    unnamed x21 -> x29, local copies, waits for them, and re-layouts: 2.45 us -> 3.89 us
    pallas_call x5 -> x4, Pallas kernels: 15.7 us -> 14.6 us  [shards(): pl.pallas_call(functools.partial(couple_kernel, first, groups, group_size...]
  transfers between devices with their start and end apart: 30 -> 27, of which waited for: 7 -> 8; matrix products, arithmetic and copies ran while one was open for 1% -> 0% of each run, Pallas kernels for 31% -> 42%
where the time goes in v1:
time: 110 us; the launch traced here: 109 us
  Pallas kernels  52.6 us (48%)
  starting transfers between devices  32 us (29%)
  waiting for transfers between devices  19.5 us (18%)
  local copies, waits for them, and re-layouts  3.9 us (4%)
    pallas_call x2, Pallas kernels, transport_inner(): pl.pallas_call(functools.partial(inner_kernel, some[0], count, blocks, TO...  15.5 us
    pallas_call x4, Pallas kernels, transport_outer(): pl.pallas_call(functools.partial(outer_kernel, some, tuple((len(h) for h...  14.9 us
    pallas_call x4, Pallas kernels, shards(): pl.pallas_call(functools.partial(couple_kernel, first, groups, group_size...  14.6 us
    ppermute x4, starting transfers between devices, hopped(): return lax.ppermute(array, 'space', pairs)  14.4 us
    ppermute x18, waiting for transfers between devices, exchange(): lax.ppermute(parts[k], 'sec', [(i, i ^ k) for i in range(groups)])  13.2 us
    ppermute x18, starting transfers between devices, exchange(): lax.ppermute(parts[k], 'sec', [(i, i ^ k) for i in range(groups)])  10.6 us
    ppermute x5, starting transfers between devices, swapped(): return lax.ppermute(array, 'space', swap)  7.11 us
    ppermute x5, waiting for transfers between devices, swapped(): return lax.ppermute(array, 'space', swap)  6.31 us
  transfers between devices with their start and end apart: 27, of which 8 were waited for; matrix products, arithmetic and copies ran while one was open for 0% of the time, Pallas kernels for 42%

profile of v1, /device:TPU:0, one launch (start us, length us, event | category | flops | bytes accessed | tf_op | source)
XLA Modules:
  0.0 109.1 jit_solution(1025150235922998973)
XLA Ops:
  0.6 0.8 copy-done.4
  1.5 0.8 copy-done.5
  2.3 0.7 copy-done.6
  3.0 3.2 %select_upwind_rows.2 = (f32[18,64,128]{2,1,0:T(8,128)S(1)}, f32[16,128,128]{2,1,0:T(8,128)}, f32[128,128]{1,0:T(8,128)S(1)}) custom-call(f32[16]{0:T(128)S(1)} %copy-done.6, f32[16,640,128]{2,1,0:T(8,128)} %bitcast.27, f32[16,640,128]{2,1,0:T(8,128)} %bitcast.28, f32[16,640,128]{2,1,0:T(8,128)} %bitcast.29, s32[128,128]{1,0:T(8,128)S(1)} %bitcast.25, ...), custom_call_target="tpu_custom_call" | custom-call | flops 1310720 | bytes 4718592 | tf_op jit(solution)/shard_map/select_upwind_rows/pallas_call | solution.py:448
  6.2 3.0 %collective-permute-start.4 = (f32[18,64,128]{2,1,0:T(8,128)S(1)}, f32[18,64,128]{2,1,0:T(8,128)S(1)}, u32[]{:S(2)}, u32[]{:S(2)}) collective-permute-start(f32[18,64,128]{2,1,0:T(8,128)S(1)} %get-tuple-element.60._), channel_id=1, source_target_pairs={{0,1},{1,0},{2,3},{3,2},{4,5},{5,4},{6,7},{7,6},{8,9},{9,8},{10,11... | collective-permute-start | bytes 1769480 | tf_op jit(solution)/shard_map/ppermute | solution.py:528
  9.2 1.3 %collective-permute-start = (f32[16,128,128]{2,1,0:T(8,128)}, f32[16,128,128]{2,1,0:T(8,128)}, u32[]{:S(2)}, u32[]{:S(2)}) collective-permute-start(f32[16,128,128]{2,1,0:T(8,128)} %get-tuple-element.65.own_ref), channel_id=1, source_target_pairs={{2,0},{4,2},{6,4},{1,3},{3,5},{5,7},{10,8},{12,10},{14,12},{9,11},... | collective-permute-start | bytes 3145736 | tf_op jit(solution)/shard_map/ppermute | solution.py:531
  10.6 7.0 %transport_inner_rows.2 = (f32[16,32,128]{2,1,0:T(8,128)S(1)}, f32[16,32,128]{2,1,0:T(8,128)S(1)}, f32[16,32,128]{2,1,0:T(8,128)S(1)}, f32[16,32,128]{2,1,0:T(8,128)S(1)}) custom-call(s32[1]{0:T(128)} %bitcast.me_ref.refs_0_, f32[16]{0:T(128)S(1)} %copy-done.7, f32[16]{0:T(128)S(1)} %copy-done.8, f32[16,5]{1,0:T(8,128)S(1)} %copy.21.inflow_ref, ...), custom_call_target="tpu_custom_call" | custom-call | flops 10485760 | bytes 2621440 | tf_op jit(solution)/shard_map/transport_inner_rows/pallas_call | solution.py:465
  17.7 1.6 %collective-permute-start.2 = (f32[16,32,128]{2,1,0:T(8,128)S(1)}, f32[16,32,128]{2,1,0:T(8,128)S(1)}, u32[]{:S(2)}, u32[]{:S(2)}) collective-permute-start(f32[16,32,128]{2,1,0:T(8,128)S(1)} %get-tuple-element.68), channel_id=1, source_target_pairs={{0,16},{8,24},{16,0},{24,8},{1,17},{9,25},{17,1},{25,9},{2,18},{10... | collective-permute-start | bytes 786440 | tf_op jit(solution)/shard_map/ppermute | solution.py:418
  19.3 0.3 collective-permute-start.3
  19.6 2.5 %select_upwind_rows.3 = (f32[16,64,128]{2,1,0:T(8,128)S(1)}, f32[16,64,128]{2,1,0:T(8,128)}) custom-call(f32[16]{0:T(128)S(1)} %copy-done.7, f32[16,640,128]{2,1,0:T(8,128)} %bitcast.32, f32[16,640,128]{2,1,0:T(8,128)} %bitcast.33, f32[16,32,128]{2,1,0:T(8,128)S(1)} %get-tuple-element.62.refs_2_.refs_8_), custom_call_target="tpu_custom_call" | custom-call | flops 1310720 | bytes 3145728 | tf_op jit(solution)/shard_map/select_upwind_rows/pallas_call | solution.py:448
  22.1 0.4 collective-permute-done.4.near_ref.rest_1_
  22.6 3.2 %collective-permute-start.12 = (f32[16,64,128]{2,1,0:T(8,128)S(1)}, f32[16,64,128]{2,1,0:T(8,128)}, u32[]{:S(2)}, u32[]{:S(2)}) collective-permute-start(f32[16,64,128]{2,1,0:T(8,128)S(1)} %get-tuple-element.63._), channel_id=1, source_target_pairs={{0,1},{1,0},{2,3},{3,2},{4,5},{5,4},{6,7},{7,6},{8,9},{9,8},{10,11... | collective-permute-start | bytes 1572872 | tf_op jit(solution)/shard_map/ppermute | solution.py:528
  25.9 1.0 collective-permute-done.2.refs_10_
  26.9 0.7 copy-done
  27.6 4.6 %collective-permute-start.5 = (f32[18,64,128]{2,1,0:T(8,128)S(1)}, f32[18,64,128]{2,1,0:T(8,128)S(1)}, u32[]{:S(2)}, u32[]{:S(2)}) collective-permute-start(f32[18,64,128]{2,1,0:T(8,128)S(1)} %collective-permute-done.4.near_ref.rest_1_), channel_id=1, source_target_pairs={{0,2},{2,4},{4,6},{3,1},{5,3},{7,5},{8,10},{10,12},{12,14},{11,9},... | collective-permute-start | bytes 1769480 | tf_op jit(solution)/shard_map/ppermute | solution.py:531
  32.2 8.5 %transport_inner_rows.3 = (f32[16,48,128]{2,1,0:T(8,128)S(1)}, f32[16,48,128]{2,1,0:T(8,128)}, f32[16,48,128]{2,1,0:T(8,128)}, f32[16,48,128]{2,1,0:T(8,128)S(1)}) custom-call(s32[1]{0:T(128)} %bitcast.me_ref.refs_0_, f32[16]{0:T(128)S(1)} %copy-done.7, f32[16]{0:T(128)S(1)} %copy-done.8, f32[16,5]{1,0:T(8,128)S(1)} %copy.21.inflow_ref, ...), custom_call_target="tpu_custom_call" | custom-call | flops 15728640 | bytes 3932160 | tf_op jit(solution)/shard_map/transport_inner_rows/pallas_call | solution.py:465
  40.7 0.7 copy-done.2
  41.4 0.1 collective-permute-start.8
  41.5 4.2 %collective-permute-start.13 = (f32[16,64,128]{2,1,0:T(8,128)}, f32[16,64,128]{2,1,0:T(8,128)}, u32[]{:S(2)}, u32[]{:S(2)}) collective-permute-start(f32[16,64,128]{2,1,0:T(8,128)} %collective-permute-done.12.rest_1_), channel_id=1, source_target_pairs={{0,2},{2,4},{4,6},{3,1},{5,3},{7,5},{8,10},{10,12},{12,14},{11,9},... | collective-permute-start | bytes 1572872 | tf_op jit(solution)/shard_map/ppermute | solution.py:531
  45.8 7.0 %collective-permute-done.8.refs_11_ = f32[16,48,128]{2,1,0:T(8,128)S(1)} collective-permute-done((f32[16,48,128]{2,1,0:T(8,128)S(1)}, f32[16,48,128]{2,1,0:T(8,128)S(1)}, u32[]{:S(2)}, u32[]{:S(2)}) %collective-permute-start.8) | collective-permute-done | bytes 393248 | tf_op jit(solution)/shard_map/ppermute | solution.py:418
  52.8 0.7 collective-permute-start.7
  53.5 1.9 %relay_upwind_rows.1 = (f32[16,64,128]{2,1,0:T(8,128)S(1)}, f32[16,64,128]{2,1,0:T(8,128)S(1)}) custom-call(s32[1]{0:T(128)} %bitcast.4.odd_ref, f32[16]{0:T(128)S(1)} %copy-done.7, f32[16,48,128]{2,1,0:T(8,128)S(1)} %get-tuple-element.72._.refs_8_, f32[16,128,128]{2,1,0:T(8,128)} %get-tuple-element.65.own_ref, f32[16,128,128]{2,1,0:T(8,128)} %collective-permute-done.far_ref), custom_call_target="tpu_custom_call" | custom-call | bytes 3145728 | tf_op jit(solution)/shard_map/relay_upwind_rows/pallas_call | solution.py:513
  55.5 0.7 collective-permute-start.16
  56.2 4.3 %collective-permute-start.15 = (f32[16,64,128]{2,1,0:T(8,128)}, f32[16,64,128]{2,1,0:T(8,128)S(1)}, u32[]{:S(2)}, u32[]{:S(2)}) collective-permute-start(f32[16,64,128]{2,1,0:T(8,128)} %collective-permute-done.14.rest_2_), channel_id=1, source_target_pairs={{0,2},{2,4},{4,6},{3,1},{5,3},{7,5},{8,10},{10,12},{12,14},{11,9},... | collective-permute-start | bytes 1572872 | tf_op jit(solution)/shard_map/ppermute | solution.py:531
  60.5 3.3 %transport_outer_rows.4 = (f32[17,16,128]{2,1,0:T(8,128)S(1)}, f32[17,16,128]{2,1,0:T(8,128)S(1)}, f32[17,16,128]{2,1,0:T(8,128)S(1)}, f32[17,16,128]{2,1,0:T(8,128)S(1)}) custom-call(s32[1]{0:T(128)} %bitcast.me_ref.refs_0_, s32[1]{0:T(128)} %bitcast.4.odd_ref, f32[16]{0:T(128)S(1)} %copy-done.7, f32[16]{0:T(128)S(1)} %copy-done.8, ...), custom_call_target="tpu_custom_call" | custom-call | flops 5242880 | bytes 2621440 | tf_op jit(solution)/shard_map/transport_outer_rows/pallas_call | solution.py:486
  63.8 0.3 collective-permute-done.7.refs_10_
  64.1 0.6 collective-permute-start.11
  64.8 0.8 collective-permute-start.10
  65.5 0.5 collective-permute-start.9
  66.0 3.4 %transport_outer_rows.5 = (f32[16,16,128]{2,1,0:T(8,128)S(1)}, f32[16,16,128]{2,1,0:T(8,128)S(1)}, f32[16,16,128]{2,1,0:T(8,128)S(1)}, f32[16,16,128]{2,1,0:T(8,128)S(1)}) custom-call(s32[1]{0:T(128)} %bitcast.me_ref.refs_0_, s32[1]{0:T(128)} %bitcast.4.odd_ref, f32[16]{0:T(128)S(1)} %copy-done.7, f32[16]{0:T(128)S(1)} %copy-done.8, ...), custom_call_target="tpu_custom_call" | custom-call | flops 5242880 | bytes 2621440 | tf_op jit(solution)/shard_map/transport_outer_rows/pallas_call | solution.py:486
  69.5 0.7 collective-permute-done.11.refs_7_.refs_15_
  70.1 2.8 %collective-permute-done.10.refs_6_.refs_14_ = f32[17,16,128]{2,1,0:T(8,128)S(1)} collective-permute-done((f32[17,16,128]{2,1,0:T(8,128)S(1)}, f32[17,16,128]{2,1,0:T(8,128)S(1)}, u32[]{:S(2)}, u32[]{:S(2)}) %collective-permute-start.10) | collective-permute-done | bytes 139296 | tf_op jit(solution)/shard_map/ppermute | solution.py:418
  72.9 0.1 collective-permute-start.17
  73.1 1.1 %collective-permute-start.18 = (f32[16,16,128]{2,1,0:T(8,128)S(1)}, f32[16,16,128]{2,1,0:T(8,128)S(1)}, u32[]{:S(2)}, u32[]{:S(2)}) collective-permute-start(f32[16,16,128]{2,1,0:T(8,128)S(1)} %get-tuple-element.95), channel_id=1, source_target_pairs={{0,16},{8,24},{16,0},{24,8},{1,17},{9,25},{17,1},{25,9},{2,18},{10... | collective-permute-start | bytes 393224 | tf_op jit(solution)/shard_map/ppermute | solution.py:418
  74.2 0.6 collective-permute-start.19
  74.9 4.8 %transport_outer_rows.6 = (f32[16,32,128]{2,1,0:T(8,128)S(1)}, f32[16,32,128]{2,1,0:T(8,128)S(1)}, f32[16,32,128]{2,1,0:T(8,128)S(1)}, f32[16,32,128]{2,1,0:T(8,128)S(1)}) custom-call(s32[1]{0:T(128)} %bitcast.me_ref.refs_0_, s32[1]{0:T(128)} %bitcast.4.odd_ref, f32[16]{0:T(128)S(1)} %copy-done.7, f32[16]{0:T(128)S(1)} %copy-done.8, ...), custom_call_target="tpu_custom_call" | custom-call | flops 10485760 | bytes 5242880 | tf_op jit(solution)/shard_map/transport_outer_rows/pallas_call | solution.py:486
  79.7 1.4 %collective-permute-done.19.refs_15_ = f32[16,16,128]{2,1,0:T(8,128)S(1)} collective-permute-done((f32[16,16,128]{2,1,0:T(8,128)S(1)}, f32[16,16,128]{2,1,0:T(8,128)S(1)}, u32[]{:S(2)}, u32[]{:S(2)}) %collective-permute-start.19) | collective-permute-done | bytes 131104 | tf_op jit(solution)/shard_map/ppermute | solution.py:418
  81.1 0.7 collective-permute-start.24
  81.8 1.3 %collective-permute-start.25 = (f32[16,32,128]{2,1,0:T(8,128)S(1)}, f32[16,32,128]{2,1,0:T(8,128)S(1)}, u32[]{:S(2)}, u32[]{:S(2)}) collective-permute-start(f32[16,32,128]{2,1,0:T(8,128)S(1)} %get-tuple-element.109), channel_id=1, source_target_pairs={{0,16},{8,24},{16,0},{24,8},{1,17},{9,25},{17,1},{25,9},{2,18},{10... | collective-permute-start | bytes 786440 | tf_op jit(solution)/shard_map/ppermute | solution.py:418
  83.1 0.1 collective-permute-start.26
  83.2 5.8 %collective-permute-done.20.rest_1_ = f32[16,64,128]{2,1,0:T(8,128)S(1)} collective-permute-done((f32[16,64,128]{2,1,0:T(8,128)S(1)}, f32[16,64,128]{2,1,0:T(8,128)S(1)}, u32[]{:S(2)}, u32[]{:S(2)}) %collective-permute-start.20) | collective-permute-done | bytes 524320 | tf_op jit(solution)/shard_map/ppermute | solution.py:528
  89.1 3.3 %transport_outer_rows.7 = (f32[16,16,128]{2,1,0:T(8,128)S(1)}, f32[16,16,128]{2,1,0:T(8,128)S(1)}, f32[16,16,128]{2,1,0:T(8,128)S(1)}, f32[16,16,128]{2,1,0:T(8,128)S(1)}) custom-call(s32[1]{0:T(128)} %bitcast.me_ref.refs_0_, s32[1]{0:T(128)} %bitcast.4.odd_ref, f32[16]{0:T(128)S(1)} %copy-done.7, f32[16]{0:T(128)S(1)} %copy-done.8, ...), custom_call_target="tpu_custom_call" | custom-call | flops 5242880 | bytes 2621440 | tf_op jit(solution)/shard_map/transport_outer_rows/pallas_call | solution.py:486
  92.4 1.1 %collective-permute-start.22 = (f32[16,16,128]{2,1,0:T(8,128)S(1)}, f32[16,16,128]{2,1,0:T(8,128)S(1)}, u32[]{:S(2)}, u32[]{:S(2)}) collective-permute-start(f32[16,16,128]{2,1,0:T(8,128)S(1)} %get-tuple-element.103), channel_id=1, source_target_pairs={{0,16},{8,24},{16,0},{24,8},{1,17},{9,25},{17,1},{25,9},{2,18},{10... | collective-permute-start | bytes 393224 | tf_op jit(solution)/shard_map/ppermute | solution.py:418
  93.6 0.7 collective-permute-start.23
  94.5 3.4 %couple_sections.4 = (f32[64,5,8,512]{3,2,1,0:T(8,128)}, f32[5,8,512]{2,1,0:T(8,128)}, f32[8,64,512]{2,1,0:T(8,128)S(1)}) custom-call(s32[1]{0:T(128)} %bitcast.me_ref.refs_0_, f32[64]{0:T(128)S(1)} %copy-done.9, bf16[64,192]{1,0:T(8,128)(2,1)S(1)} %pad_maximum_fusion.refs_2_, f32[32,128]{1,0:T(8,128)S(1)} %bitcast.21, ...), custom_call_target="tpu_custom_call" | custom-call | flops 33554432 | bytes 3145728 | tf_op jit(solution)/shard_map/couple_sections/pallas_call | solution.py:616
  97.9 3.1 %couple_sections.5 = (f32[64,5,8,512]{3,2,1,0:T(8,128)}, f32[5,8,512]{2,1,0:T(8,128)}) custom-call(s32[1]{0:T(128)} %bitcast.me_ref.refs_0_, f32[64]{0:T(128)S(1)} %copy-done.9, bf16[64,192]{1,0:T(8,128)(2,1)S(1)} %pad_maximum_fusion.refs_2_, f32[32,128]{1,0:T(8,128)S(1)} %bitcast.22, ...), custom_call_target="tpu_custom_call", output_to_operand_aliasing={{0}: (17, {}), {1}: (18, {})} | custom-call | flops 33554432 | bytes 3145728 | tf_op jit(solution)/shard_map/couple_sections/pallas_call | solution.py:616
  101.0 5.0 %couple_sections.6 = (f32[64,5,8,512]{3,2,1,0:T(8,128)}, f32[5,8,512]{2,1,0:T(8,128)}) custom-call(s32[1]{0:T(128)} %bitcast.me_ref.refs_0_, f32[64]{0:T(128)S(1)} %copy-done.9, bf16[64,192]{1,0:T(8,128)(2,1)S(1)} %pad_maximum_fusion.refs_2_, f32[32,128]{1,0:T(8,128)S(1)} %bitcast.23, ...), custom_call_target="tpu_custom_call", output_to_operand_aliasing={{0}: (17, {}), {1}: (18, {})} | custom-call | flops 67108864 | bytes 6291456 | tf_op jit(solution)/shard_map/couple_sections/pallas_call | solution.py:616
  106.0 3.1 %couple_sections.7 = (f32[64,5,8,512]{3,2,1,0:T(8,128)}, f32[5,8,512]{2,1,0:T(8,128)}) custom-call(s32[1]{0:T(128)} %bitcast.me_ref.refs_0_, f32[64]{0:T(128)S(1)} %copy-done.9, bf16[64,192]{1,0:T(8,128)(2,1)S(1)} %pad_maximum_fusion.refs_2_, f32[32,128]{1,0:T(8,128)S(1)} %bitcast.24, ...), custom_call_target="tpu_custom_call", output_to_operand_aliasing={{0}: (17, {}), {1}: (18, {})} | custom-call | flops 33554432 | bytes 3145728 | tf_op jit(solution)/shard_map/couple_sections/pallas_call | solution.py:616
  (53 shorter events, 0.6 us)
Async XLA Ops:
  0.6 0.8 copy-start.4
  1.5 0.8 copy-start.5
  2.3 0.7 copy-start.6
  3.0 7.6 %copy-start.13 = (f32[16,5]{0,1:T(8,128)S(1)}, f32[16,5]{0,1:T(8,128)}, u32[]{:S(2)}) copy-start(f32[16,5]{0,1:T(8,128)} %param.13) | copy-start | bytes 964
  3.0 7.7 %copy-start.7 = (f32[16]{0:T(128)S(1)}, f32[16]{0:T(128)}, u32[]{:S(2)}) copy-start(f32[16]{0:T(128)} %ux_ref.17) | copy-start | bytes 196
  3.0 7.7 %copy-start.8 = (f32[16]{0:T(128)S(1)}, f32[16]{0:T(128)}, u32[]{:S(2)}) copy-start(f32[16]{0:T(128)} %uy_ref.11) | copy-start | bytes 196
  6.2 16.4 %collective-permute-start.4 = (f32[18,64,128]{2,1,0:T(8,128)S(1)}, f32[18,64,128]{2,1,0:T(8,128)S(1)}, u32[]{:S(2)}, u32[]{:S(2)}) collective-permute-start(f32[18,64,128]{2,1,0:T(8,128)S(1)} %get-tuple-element.60._), channel_id=1, source_target_pairs={{0,1},{1,0},{2,3},{3,2},{4,5},{5,4},{6,7},{7,6},{8,9},{9,8},{10,11... | collective-permute-start | bytes 1769480 | tf_op jit(solution)/shard_map/ppermute | solution.py:528
  9.2 44.3 %collective-permute-start = (f32[16,128,128]{2,1,0:T(8,128)}, f32[16,128,128]{2,1,0:T(8,128)}, u32[]{:S(2)}, u32[]{:S(2)}) collective-permute-start(f32[16,128,128]{2,1,0:T(8,128)} %get-tuple-element.65.own_ref), channel_id=1, source_target_pairs={{2,0},{4,2},{6,4},{1,3},{3,5},{5,7},{10,8},{12,10},{14,12},{9,11},... | collective-permute-start | bytes 3145736 | tf_op jit(solution)/shard_map/ppermute | solution.py:531
  17.7 8.2 %collective-permute-start.1 = (f32[16,32,128]{2,1,0:T(8,128)S(1)}, f32[16,32,128]{2,1,0:T(8,128)S(1)}, u32[]{:S(2)}, u32[]{:S(2)}) collective-permute-start(f32[16,32,128]{2,1,0:T(8,128)S(1)} %get-tuple-element.67), channel_id=1, source_target_pairs={{0,8},{8,0},{16,24},{24,16},{1,9},{9,1},{17,25},{25,17},{2,10},{10... | collective-permute-start | bytes 786440 | tf_op jit(solution)/shard_map/ppermute | solution.py:418
  17.7 9.2 %collective-permute-start.2 = (f32[16,32,128]{2,1,0:T(8,128)S(1)}, f32[16,32,128]{2,1,0:T(8,128)S(1)}, u32[]{:S(2)}, u32[]{:S(2)}) collective-permute-start(f32[16,32,128]{2,1,0:T(8,128)S(1)} %get-tuple-element.68), channel_id=1, source_target_pairs={{0,16},{8,24},{16,0},{24,8},{1,17},{9,25},{17,1},{25,9},{2,18},{10... | collective-permute-start | bytes 786440 | tf_op jit(solution)/shard_map/ppermute | solution.py:418
  19.3 21.4 %collective-permute-start.3 = (f32[16,32,128]{2,1,0:T(8,128)S(1)}, f32[16,32,128]{2,1,0:T(8,128)S(1)}, u32[]{:S(2)}, u32[]{:S(2)}) collective-permute-start(f32[16,32,128]{2,1,0:T(8,128)S(1)} %get-tuple-element.69), channel_id=1, source_target_pairs={{0,24},{8,16},{16,8},{24,0},{1,25},{9,17},{17,9},{25,1},{2,26},{10... | collective-permute-start | bytes 786440 | tf_op jit(solution)/shard_map/ppermute | solution.py:418
  22.6 19.0 %collective-permute-start.12 = (f32[16,64,128]{2,1,0:T(8,128)S(1)}, f32[16,64,128]{2,1,0:T(8,128)}, u32[]{:S(2)}, u32[]{:S(2)}) collective-permute-start(f32[16,64,128]{2,1,0:T(8,128)S(1)} %get-tuple-element.63._), channel_id=1, source_target_pairs={{0,1},{1,0},{2,3},{3,2},{4,5},{5,4},{6,7},{7,6},{8,9},{9,8},{10,11... | collective-permute-start | bytes 1572872 | tf_op jit(solution)/shard_map/ppermute | solution.py:528
  25.8 29.6 %collective-permute-start.14 = (f32[16,64,128]{2,1,0:T(8,128)}, f32[16,64,128]{2,1,0:T(8,128)}, u32[]{:S(2)}, u32[]{:S(2)}) collective-permute-start(f32[16,64,128]{2,1,0:T(8,128)} %get-tuple-element.89), channel_id=1, source_target_pairs={{0,1},{1,0},{2,3},{3,2},{4,5},{5,4},{6,7},{7,6},{8,9},{9,8},{10,11... | collective-permute-start | bytes 1572872 | tf_op jit(solution)/shard_map/ppermute | solution.py:528
  26.9 0.7 copy-start
  27.6 28.5 %collective-permute-start.5 = (f32[18,64,128]{2,1,0:T(8,128)S(1)}, f32[18,64,128]{2,1,0:T(8,128)S(1)}, u32[]{:S(2)}, u32[]{:S(2)}) collective-permute-start(f32[18,64,128]{2,1,0:T(8,128)S(1)} %collective-permute-done.4.near_ref.rest_1_), channel_id=1, source_target_pairs={{0,2},{2,4},{4,6},{3,1},{5,3},{7,5},{8,10},{10,12},{12,14},{11,9},... | collective-permute-start | bytes 1769480 | tf_op jit(solution)/shard_map/ppermute | solution.py:531
  40.7 0.7 copy-start.2
  41.4 11.4 %collective-permute-start.8 = (f32[16,48,128]{2,1,0:T(8,128)S(1)}, f32[16,48,128]{2,1,0:T(8,128)S(1)}, u32[]{:S(2)}, u32[]{:S(2)}) collective-permute-start(f32[16,48,128]{2,1,0:T(8,128)S(1)} %get-tuple-element.78), channel_id=1, source_target_pairs={{0,24},{8,16},{16,8},{24,0},{1,25},{9,17},{17,9},{25,1},{2,26},{10... | collective-permute-start | bytes 1179656 | tf_op jit(solution)/shard_map/ppermute | solution.py:418
  41.5 24.0 %collective-permute-start.13 = (f32[16,64,128]{2,1,0:T(8,128)}, f32[16,64,128]{2,1,0:T(8,128)}, u32[]{:S(2)}, u32[]{:S(2)}) collective-permute-start(f32[16,64,128]{2,1,0:T(8,128)} %collective-permute-done.12.rest_1_), channel_id=1, source_target_pairs={{0,2},{2,4},{4,6},{3,1},{5,3},{7,5},{8,10},{10,12},{12,14},{11,9},... | collective-permute-start | bytes 1572872 | tf_op jit(solution)/shard_map/ppermute | solution.py:531
  52.8 11.3 %collective-permute-start.7 = (f32[16,48,128]{2,1,0:T(8,128)}, f32[16,48,128]{2,1,0:T(8,128)S(1)}, u32[]{:S(2)}, u32[]{:S(2)}) collective-permute-start(f32[16,48,128]{2,1,0:T(8,128)} %get-tuple-element.76), channel_id=1, source_target_pairs={{0,16},{8,24},{16,0},{24,8},{1,17},{9,25},{17,1},{25,9},{2,18},{10... | collective-permute-start | bytes 1179656 | tf_op jit(solution)/shard_map/ppermute | solution.py:418
  53.5 10.6 %collective-permute-start.6 = (f32[16,48,128]{2,1,0:T(8,128)}, f32[16,48,128]{2,1,0:T(8,128)S(1)}, u32[]{:S(2)}, u32[]{:S(2)}) collective-permute-start(f32[16,48,128]{2,1,0:T(8,128)} %get-tuple-element.74), channel_id=1, source_target_pairs={{0,8},{8,0},{16,24},{24,16},{1,9},{9,1},{17,25},{25,17},{2,10},{10... | collective-permute-start | bytes 1179656 | tf_op jit(solution)/shard_map/ppermute | solution.py:418
  55.5 19.3 %collective-permute-start.16 = (f32[16,64,128]{2,1,0:T(8,128)S(1)}, f32[16,64,128]{2,1,0:T(8,128)S(1)}, u32[]{:S(2)}, u32[]{:S(2)}) collective-permute-start(f32[16,64,128]{2,1,0:T(8,128)S(1)} %get-tuple-element.90._), channel_id=1, source_target_pairs={{0,1},{1,0},{2,3},{3,2},{4,5},{5,4},{6,7},{7,6},{8,9},{9,8},{10,11... | collective-permute-start | bytes 1572872 | tf_op jit(solution)/shard_map/ppermute | solution.py:528
  56.2 18.7 %collective-permute-start.15 = (f32[16,64,128]{2,1,0:T(8,128)}, f32[16,64,128]{2,1,0:T(8,128)S(1)}, u32[]{:S(2)}, u32[]{:S(2)}) collective-permute-start(f32[16,64,128]{2,1,0:T(8,128)} %collective-permute-done.14.rest_2_), channel_id=1, source_target_pairs={{0,2},{2,4},{4,6},{3,1},{5,3},{7,5},{8,10},{10,12},{12,14},{11,9},... | collective-permute-start | bytes 1572872 | tf_op jit(solution)/shard_map/ppermute | solution.py:531
  64.1 6.0 %collective-permute-start.11 = (f32[17,16,128]{2,1,0:T(8,128)S(1)}, f32[17,16,128]{2,1,0:T(8,128)S(1)}, u32[]{:S(2)}, u32[]{:S(2)}) collective-permute-start(f32[17,16,128]{2,1,0:T(8,128)S(1)} %get-tuple-element.85), channel_id=1, source_target_pairs={{0,24},{8,16},{16,8},{24,0},{1,25},{9,17},{17,9},{25,1},{2,26},{10... | collective-permute-start | bytes 417800 | tf_op jit(solution)/shard_map/ppermute | solution.py:418
  64.8 8.2 %collective-permute-start.10 = (f32[17,16,128]{2,1,0:T(8,128)S(1)}, f32[17,16,128]{2,1,0:T(8,128)S(1)}, u32[]{:S(2)}, u32[]{:S(2)}) collective-permute-start(f32[17,16,128]{2,1,0:T(8,128)S(1)} %get-tuple-element.83), channel_id=1, source_target_pairs={{0,16},{8,24},{16,0},{24,8},{1,17},{9,25},{17,1},{25,9},{2,18},{10... | collective-permute-start | bytes 417800 | tf_op jit(solution)/shard_map/ppermute | solution.py:418
  65.5 7.4 %collective-permute-start.9 = (f32[17,16,128]{2,1,0:T(8,128)S(1)}, f32[17,16,128]{2,1,0:T(8,128)S(1)}, u32[]{:S(2)}, u32[]{:S(2)}) collective-permute-start(f32[17,16,128]{2,1,0:T(8,128)S(1)} %get-tuple-element.81), channel_id=1, source_target_pairs={{0,8},{8,0},{16,24},{24,16},{1,9},{9,1},{17,25},{25,17},{2,10},{10... | collective-permute-start | bytes 417800 | tf_op jit(solution)/shard_map/ppermute | solution.py:418
  72.9 6.8 %collective-permute-start.17 = (f32[16,16,128]{2,1,0:T(8,128)S(1)}, f32[16,16,128]{2,1,0:T(8,128)S(1)}, u32[]{:S(2)}, u32[]{:S(2)}) collective-permute-start(f32[16,16,128]{2,1,0:T(8,128)S(1)} %get-tuple-element.93), channel_id=1, source_target_pairs={{0,8},{8,0},{16,24},{24,16},{1,9},{9,1},{17,25},{25,17},{2,10},{10... | collective-permute-start | bytes 393224 | tf_op jit(solution)/shard_map/ppermute | solution.py:418
  73.1 6.7 %collective-permute-start.18 = (f32[16,16,128]{2,1,0:T(8,128)S(1)}, f32[16,16,128]{2,1,0:T(8,128)S(1)}, u32[]{:S(2)}, u32[]{:S(2)}) collective-permute-start(f32[16,16,128]{2,1,0:T(8,128)S(1)} %get-tuple-element.95), channel_id=1, source_target_pairs={{0,16},{8,24},{16,0},{24,8},{1,17},{9,25},{17,1},{25,9},{2,18},{10... | collective-permute-start | bytes 393224 | tf_op jit(solution)/shard_map/ppermute | solution.py:418
  74.2 6.9 %collective-permute-start.19 = (f32[16,16,128]{2,1,0:T(8,128)S(1)}, f32[16,16,128]{2,1,0:T(8,128)S(1)}, u32[]{:S(2)}, u32[]{:S(2)}) collective-permute-start(f32[16,16,128]{2,1,0:T(8,128)S(1)} %get-tuple-element.97), channel_id=1, source_target_pairs={{0,24},{8,16},{16,8},{24,0},{1,25},{9,17},{17,9},{25,1},{2,26},{10... | collective-permute-start | bytes 393224 | tf_op jit(solution)/shard_map/ppermute | solution.py:418
  74.8 14.3 %collective-permute-start.20 = (f32[16,64,128]{2,1,0:T(8,128)S(1)}, f32[16,64,128]{2,1,0:T(8,128)S(1)}, u32[]{:S(2)}, u32[]{:S(2)}) collective-permute-start(f32[16,64,128]{2,1,0:T(8,128)S(1)} %get-tuple-element.100), channel_id=1, source_target_pairs={{0,1},{1,0},{2,3},{3,2},{4,5},{5,4},{6,7},{7,6},{8,9},{9,8},{10,11... | collective-permute-start | bytes 1572872 | tf_op jit(solution)/shard_map/ppermute | solution.py:528
  74.8 6.9 %copy-start.10 = (f32[64,64]{1,0:T(8,128)S(1)}, f32[64,64]{1,0:T(8,128)}, u32[]{:S(2)}) copy-start(f32[64,64]{1,0:T(8,128)} %param.16) | copy-start | bytes 49156
  74.8 8.4 %copy-start.11 = (f32[64,64]{1,0:T(8,128)S(1)}, f32[64,64]{1,0:T(8,128)}, u32[]{:S(2)}) copy-start(f32[64,64]{1,0:T(8,128)} %param.17) | copy-start | bytes 49156
  79.7 14.7 %copy-start.12 = (f32[8,512]{1,0:T(8,128)S(1)}, f32[8,512]{1,0:T(8,128)}, u32[]{:S(2)}) copy-start(f32[8,512]{1,0:T(8,128)} %param.19) | copy-start | bytes 49156
  79.7 14.8 %copy-start.1 = (f32[16,32,128]{2,1,0:T(8,128)S(1)}, f32[16,32,128]{2,1,0:T(8,128)}, u32[]{:S(2)}) copy-start(f32[16,32,128]{2,1,0:T(8,128)} %copy-done) | copy-start | bytes 786436
  79.7 14.8 %copy-start.3 = (f32[16,32,128]{2,1,0:T(8,128)S(1)}, f32[16,32,128]{2,1,0:T(8,128)}, u32[]{:S(2)}) copy-start(f32[16,32,128]{2,1,0:T(8,128)} %copy-done.2) | copy-start | bytes 786436
  79.7 14.8 %copy-start.9 = (f32[64]{0:T(128)S(1)}, f32[64]{0:T(128)}, u32[]{:S(2)}) copy-start(f32[64]{0:T(128)} %refs_1_.7) | copy-start | bytes 772
  81.1 12.5 %collective-permute-start.24 = (f32[16,32,128]{2,1,0:T(8,128)S(1)}, f32[16,32,128]{2,1,0:T(8,128)S(1)}, u32[]{:S(2)}, u32[]{:S(2)}) collective-permute-start(f32[16,32,128]{2,1,0:T(8,128)S(1)} %get-tuple-element.107), channel_id=1, source_target_pairs={{0,8},{8,0},{16,24},{24,16},{1,9},{9,1},{17,25},{25,17},{2,10},{10... | collective-permute-start | bytes 786440 | tf_op jit(solution)/shard_map/ppermute | solution.py:418
  81.8 19.2 %collective-permute-start.25 = (f32[16,32,128]{2,1,0:T(8,128)S(1)}, f32[16,32,128]{2,1,0:T(8,128)S(1)}, u32[]{:S(2)}, u32[]{:S(2)}) collective-permute-start(f32[16,32,128]{2,1,0:T(8,128)S(1)} %get-tuple-element.109), channel_id=1, source_target_pairs={{0,16},{8,24},{16,0},{24,8},{1,17},{9,25},{17,1},{25,9},{2,18},{10... | collective-permute-start | bytes 786440 | tf_op jit(solution)/shard_map/ppermute | solution.py:418
  83.1 17.9 %collective-permute-start.26 = (f32[16,32,128]{2,1,0:T(8,128)S(1)}, f32[16,32,128]{2,1,0:T(8,128)S(1)}, u32[]{:S(2)}, u32[]{:S(2)}) collective-permute-start(f32[16,32,128]{2,1,0:T(8,128)S(1)} %get-tuple-element.111), channel_id=1, source_target_pairs={{0,24},{8,16},{16,8},{24,0},{1,25},{9,17},{17,9},{25,1},{2,26},{10... | collective-permute-start | bytes 786440 | tf_op jit(solution)/shard_map/ppermute | solution.py:418
  92.4 13.6 %collective-permute-start.21 = (f32[16,16,128]{2,1,0:T(8,128)S(1)}, f32[16,16,128]{2,1,0:T(8,128)S(1)}, u32[]{:S(2)}, u32[]{:S(2)}) collective-permute-start(f32[16,16,128]{2,1,0:T(8,128)S(1)} %get-tuple-element.102), channel_id=1, source_target_pairs={{0,8},{8,0},{16,24},{24,16},{1,9},{9,1},{17,25},{25,17},{2,10},{10... | collective-permute-start | bytes 393224 | tf_op jit(solution)/shard_map/ppermute | solution.py:418
  92.4 13.6 %collective-permute-start.22 = (f32[16,16,128]{2,1,0:T(8,128)S(1)}, f32[16,16,128]{2,1,0:T(8,128)S(1)}, u32[]{:S(2)}, u32[]{:S(2)}) collective-permute-start(f32[16,16,128]{2,1,0:T(8,128)S(1)} %get-tuple-element.103), channel_id=1, source_target_pairs={{0,16},{8,24},{16,0},{24,8},{1,17},{9,25},{17,1},{25,9},{2,18},{10... | collective-permute-start | bytes 393224 | tf_op jit(solution)/shard_map/ppermute | solution.py:418
  93.6 12.4 %collective-permute-start.23 = (f32[16,16,128]{2,1,0:T(8,128)S(1)}, f32[16,16,128]{2,1,0:T(8,128)S(1)}, u32[]{:S(2)}, u32[]{:S(2)}) collective-permute-start(f32[16,16,128]{2,1,0:T(8,128)S(1)} %get-tuple-element.104), channel_id=1, source_target_pairs={{0,24},{8,16},{16,8},{24,0},{1,25},{9,17},{17,9},{25,1},{2,26},{10... | collective-permute-start | bytes 393224 | tf_op jit(solution)/shard_map/ppermute | solution.py:418
